TPU v7x, 512 devices: a whole 4x4x16 slice. The times are simulated.
512 devices in a mesh: alt: 8 (over x, y_hi), strip: 64 (over z, y_lo, core).
Axes of the slice: x: 4, y: 4 (y_hi: 2, y_lo: 2; y = y_hi * 2 + y_lo), z: 16, core: 2. Of those that a mesh axis runs over, the one named last changes fastest.
Arguments:
- screens: bfloat16 [16, 512, 512], P('alt', 'strip'), may hold values from -2.390625 to 2.390625
- row_offset: int32 [2, 16, 2], replicated, may hold values from 0 to 341, as said below
- col_offset: int32 [2, 16, 2], replicated, may hold values from 0 to 341, as said below
- layer_bin: int32 [16], replicated, may hold values from 0 to 15
- illumination: float32 [16, 12800], P(None, ('alt', 'strip')), may hold values from 0.3 to 1
- reconstructor: bfloat16 [2, 12800, 6000], P(None, ('alt', 'strip')), may hold values from -0.0390625 to 0.0390625
- sat_code: int32 [6000], replicated, may hold values from 1 to 16
Outputs:
- slopes: float32 [2, 2, 12800], P(None, None, ('alt', 'strip'))
- commands: float32 [2, 6000], replicated
Inputs may be any that keep to these rules, and one draw needn't show every extreme that they name: Every footprint lies inside the screen: row_offset[f, l, g] + (319) shrink_l <= 511. Every footprint lies inside the screen: col_offset[f, l, g] + (319) shrink_l <= 511.
All inputs are finite; a program needn't handle non-finite values.
Results may differ from a plain program's by a relative error of at most 0.0028.
Values sent between devices are 32-bit elements; how exact they have to be, the bound alone decides.
No kernel may reach another device: no remote copies, remote signals or barrier semaphores. Data moves between devices by JAX's collectives and lax.ppermute only.
A program may use at most 64 MiB of HBM per device.

v0:
```python
import math

import jax
import jax.numpy as jnp
from jax import lax
from jax.sharding import PartitionSpec as P

LENSLETS = 80
PIXELS = 4
GUIDE_STARS = 2
FRAMES = 2
ACTUATORS = 6000
PUPIL_PIX = 320
WINDOW = 384
SUBAPS_ALL = 12800


highest = lax.Precision.HIGHEST
loop_gain = 0.5
code_step = 0.125
bin_step = 0.03125


def bilinear(offsets):
    return jnp.maximum(0.0, 1.0 - jnp.abs(offsets))


def dft_tables():
    padded = 2 * PIXELS
    freq_index = jnp.arange(padded * padded, dtype=jnp.int32)
    freq_row = freq_index // padded
    freq_col = freq_index % padded
    pix_index = jnp.arange(PIXELS * PIXELS, dtype=jnp.int32)
    pix_row = pix_index // PIXELS
    pix_col = pix_index % PIXELS
    turn_count = (
        freq_row[:, None] * pix_row[None, :] + freq_col[:, None] * pix_col[None, :]
    ) % padded
    angles = turn_count.astype(jnp.float32) * (2.0 * math.pi / padded)
    coord_row = ((freq_row + PIXELS) % padded - PIXELS).astype(jnp.float32)
    coord_col = ((freq_col + PIXELS) % padded - PIXELS).astype(jnp.float32)
    return (jnp.cos(angles), jnp.sin(angles), coord_row, coord_col)


def centroids(pupil_phase, illumination, tables):
    cosine, sine_table, coord_row, coord_col = tables
    field_re = illumination * jnp.cos(pupil_phase)
    field_im = illumination * jnp.sin(pupil_phase)
    real_part = jnp.dot(cosine, field_re, precision=highest) + jnp.dot(
        sine_table, field_im, precision=highest
    )
    imag_part = jnp.dot(cosine, field_im, precision=highest) - jnp.dot(
        sine_table, field_re, precision=highest
    )
    intensity = real_part * real_part + imag_part * imag_part
    flux_sum = jnp.sum(intensity, axis=0)
    slope_row = jnp.sum(intensity * coord_row[:, None], axis=0) / flux_sum
    slope_col = jnp.sum(intensity * coord_col[:, None], axis=0) / flux_sum
    return jnp.stack([slope_row, slope_col])


def shards(screens, row_offset, col_offset, layer_bin, illumination, reconstructor, sat_code):
    layer_dev = screens.shape[0]
    rows_here = screens.shape[1]
    count_here = illumination.shape[1]
    group_pos = lax.axis_index("alt")
    strip_pos = lax.axis_index("strip")
    row_global = strip_pos * rows_here + jnp.arange(rows_here, dtype=jnp.int32)
    pupil_idx = jnp.arange(PUPIL_PIX, dtype=jnp.float32)
    window_idx = jnp.arange(WINDOW, dtype=jnp.float32)
    widened_layers = [
        jnp.pad(screens[layer_no], ((0, 0), (0, WINDOW))) for layer_no in range(layer_dev)
    ]
    frame_terms = []
    for frame_no in range(FRAMES):
        running = jnp.zeros((PIXELS, PIXELS, GUIDE_STARS, LENSLETS, LENSLETS), jnp.float32)
        for layer_no in range(layer_dev):
            layer_pos = group_pos * layer_dev + layer_no
            tops = lax.dynamic_index_in_dim(row_offset[frame_no], layer_pos, 0, keepdims=False)
            lefts = lax.dynamic_index_in_dim(col_offset[frame_no], layer_pos, 0, keepdims=False)
            bin_value = lax.dynamic_index_in_dim(layer_bin, layer_pos, 0, keepdims=False)
            shrink = 1.0 - bin_value.astype(jnp.float32) * bin_step
            col_weights = bilinear(window_idx[None, :] - pupil_idx[:, None] * shrink)
            widened = widened_layers[layer_no]

            def cut_columns(left_col):
                return lax.dynamic_slice_in_dim(widened, left_col, WINDOW, 1)

            strips = jax.vmap(cut_columns)(lefts).astype(jnp.float32)
            across = jnp.einsum("drc,jc->drj", strips, col_weights, precision=highest)
            offsets = (row_global[None, :] - tops[:, None]).astype(jnp.float32)
            row_weights = bilinear(offsets[:, None, :] - pupil_idx[None, :, None] * shrink)
            running = running + jnp.einsum(
                "dapr,drbq->pqdab",
                row_weights.reshape(GUIDE_STARS, LENSLETS, PIXELS, rows_here),
                across.reshape(GUIDE_STARS, rows_here, LENSLETS, PIXELS),
                precision=highest,
            )
        frame_terms.append(running.reshape(PIXELS * PIXELS, SUBAPS_ALL))
    phase_terms = jnp.concatenate(frame_terms, axis=0)
    owned = lax.psum_scatter(phase_terms, ("alt", "strip"), scatter_dimension=1, tiled=True)
    pupil_phase = owned.reshape(FRAMES, PIXELS * PIXELS, count_here)
    tables = dft_tables()
    slopes = jnp.stack(
        [centroids(pupil_phase[frame_no], illumination, tables) for frame_no in range(FRAMES)]
    )
    rounded = slopes.astype(jnp.bfloat16).reshape(FRAMES, 2 * count_here)
    partial_value = jnp.dot(
        rounded,
        reconstructor.reshape(2 * count_here, ACTUATORS),
        preferred_element_type=jnp.float32,
    )
    updates = lax.psum(partial_value, ("alt", "strip"))
    limits = sat_code.astype(jnp.float32) * code_step
    first_cmd = jnp.clip(loop_gain * updates[0], -limits, limits)
    second_cmd = jnp.clip(first_cmd + loop_gain * updates[1], -limits, limits)
    return (slopes, jnp.stack([first_cmd, second_cmd]))


def solution(mesh):
    placed = (
        P("alt", "strip", None),
        P(),
        P(),
        P(),
        P(None, ("alt", "strip")),
        P(None, ("alt", "strip"), None),
        P(),
    )
    return jax.shard_map(
        shards,
        mesh=mesh,
        in_specs=placed,
        out_specs=(P(None, None, ("alt", "strip")), P()),
        check_vma=False,
    )
```

profile of v0, /device:TPU:1, one launch (start us, length us, event | category | flops | bytes accessed | tf_op | source)
XLA Modules:
  0.0 635.3 jit_solution(2373824298019678638)
XLA Ops:
  7.2 0.0 all-reduce.9.cloned.1.call-start
  7.2 1.4 fusion.161
  10.0 0.7 fusion.159
  10.8 0.7 fusion.160
  11.4 0.2 fusion.102
  11.7 0.1 copy.79
  11.8 0.1 concatenate.15.clone
  11.8 0.7 slice_bitcast_fusion
  12.6 2.7 while.4
  12.6 0.6 slice.108
  13.2 0.7 bitcast_dynamic-update-slice_fusion.8
  13.9 0.6 slice.108
  14.6 0.7 bitcast_dynamic-update-slice_fusion.8
  15.3 0.1 copy.80
  15.4 0.1 concatenate.16.clone
  15.5 2.5 while.5
  15.5 0.6 slice.109
  16.0 0.6 bitcast_dynamic-update-slice_fusion.9
  16.7 0.6 slice.109
  17.3 0.6 bitcast_dynamic-update-slice_fusion.9
  17.9 0.2 fusion.103
  18.1 0.5 fusion.15
  18.7 0.5 fusion.11
  19.2 0.1 subtract_convert_fusion.2
  19.2 1.2 fusion.21
  20.5 1.2 fusion.1
  21.7 0.4 copy.45
  22.1 1.7 reshape.445
  23.8 0.2 fusion.106
  24.0 0.1 copy.81
  24.1 0.1 concatenate.17.clone
  24.2 2.7 while.6
  24.2 0.6 slice.110
  24.8 0.7 bitcast_dynamic-update-slice_fusion.10
  25.6 0.6 slice.110
  26.2 0.7 bitcast_dynamic-update-slice_fusion.10
  26.9 0.5 fusion.13
  27.4 0.1 copy.82
  27.5 0.1 concatenate.18.clone
  27.6 2.6 while.7
  27.6 0.6 slice.111
  28.2 0.7 bitcast_dynamic-update-slice_fusion.11
  28.9 0.6 slice.111
  29.5 0.7 bitcast_dynamic-update-slice_fusion.11
  30.2 0.5 fusion.9
  30.8 1.2 fusion.18
  32.0 1.2 fusion
  33.2 0.4 copy.52
  33.7 1.7 reshape.448
  35.4 2.5 pad_maximum_fusion
  38.0 477.4 %all-reduce.9.cloned.1.call-done = f32[32,12800]{1,0:T(8,128)} async-done(((f32[32,12800]{1,0:T(8,128)}), f32[32,12800]{1,0:T(8,128)}) %all-reduce.9.cloned.1.call-update) | async-done | bytes 1638416
  515.4 1.1 fusion.84
  516.5 1.1 fusion.82
  517.6 1.1 fusion.80
  518.7 1.1 fusion.78
  519.9 1.1 fusion.4
  521.0 1.1 fusion.7
  522.2 1.1 fusion.6
  523.3 1.3 multiply_reduce_fusion.1
  524.7 0.3 convolution_bitcast_fusion
  525.0 102.0 %psum.7 = f32[2,6000]{1,0:T(2,128)S(1)} all-reduce(f32[2,6000]{1,0:T(2,128)S(1)} %convolution_bitcast_fusion), channel_id=1, replica_groups=mesh['alt'=8,'strip'=64] {'alt','strip'}, use_global_device_ids=true, to_apply=%region_7.8 | all-reduce | flops 12000 | bytes 96000 | tf_op jit(solution)/shard_map/psum | solution.py:113
  627.0 0.1 fusion.59
  627.2 0.6 copy.56
  627.8 0.7 pad_maximum_fusion.1
  (41 shorter events, 0.3 us)
Async XLA Ops:
  7.2 517.5 %copy-start = (bf16[2,25,6000]{2,0,1:T(2,128)(2,1)S(1)}, bf16[2,25,6000]{2,0,1:T(2,128)(2,1)}, u32[]{:S(2)}) copy-start(bf16[2,25,6000]{2,0,1:T(2,128)(2,1)} %param.12) | copy-start | bytes 1800004
  7.2 508.2 %all-reduce.9.cloned.1.call-start = ((), (), s32[]{:S(2)}) async-start(), calls=%async_computation | async-start | bytes 3276800
  33.6 1.7 copy-start.1
  37.9 477.5 %copy-start.3 = (f32[16,25]{1,0:T(8,128)S(1)}, f32[16,25]{1,0:T(8,128)}, u32[]{:S(2)}) copy-start(f32[16,25]{1,0:T(8,128)} %param.11) | copy-start | bytes 4804
  37.9 589.2 %copy-start.2 = (s32[6000]{0:T(1024)S(1)}, s32[6000]{0:T(1024)}, u32[]{:S(2)}) copy-start(s32[6000]{0:T(1024)} %param.13) | copy-start | bytes 72004
Sparse Core Ops, SparseCore 0:
  38.0 477.3 all-reduce.8
where the time goes:
time: 636 us; the launch traced here: 635 us
  waiting for transfers between devices  477 us (75%)
  blocking collectives  102 us (16%)
  local copies, waits for them, and re-layouts  20.2 us (3%)
  matrix products  16.4 us (3%)
  between operations  15.7 us (2%)
    unnamed x2, waiting for transfers between devices  477 us
    psum x1, blocking collectives, shards(): updates = lax.psum(partial_value, ('alt', 'strip'))  102 us
  transfers between devices with their start and end apart: 1, of which 1 were waited for; matrix products, arithmetic and copies ran while one was open for 0% of the time, Pallas kernels for 0%

commit v1 on v0

v1 whole, which is shorter than its diff:
```python
import jax
import jax.numpy as jnp
from jax import lax
from jax.experimental import pallas as pl
from jax.experimental.pallas import tpu as pltpu
from jax.sharding import Mesh, PartitionSpec as P

ACTUATORS = 6000
F32 = jnp.float32
BF16 = jnp.bfloat16
I32 = jnp.int32

NAMES = ("xh", "xl", "yh", "zh", "zl", "yl", "co")
SIZES = (2, 2, 2, 4, 4, 2, 2)
ALT = ("xh", "xl", "yh")
STRIP = ("zh", "zl", "yl", "co")
PLANE = ("xh", "xl", "yh", "yl", "co")
HALF = ("xl", "yh", "yl", "co")
RING = ("zh", "zl")

ROOT = 2.0**0.5
LAG = (2.0 + 2.0 * ROOT, -2.0, 2.0 * ROOT - 2.0)

SMEM = pl.BlockSpec(memory_space=pltpu.SMEM)
VMEM = pl.BlockSpec(memory_space=pltpu.VMEM)


def iota(shape, dim):
    return lax.broadcasted_iota(I32, shape, dim)


def alt_index():
    return lax.axis_index("xh") * 4 + lax.axis_index("xl") * 2 + lax.axis_index("yh")


def ylc_index():
    return lax.axis_index("yl") * 2 + lax.axis_index("co")


def block_index():
    return (lax.axis_index("xl") * 2 + lax.axis_index("yh")) * 4 + ylc_index()


def columns_kernel(col_ref, bin_ref, screen_ref, out_ref):
    alt = alt_index()
    lane = iota((1, 512), 1)
    column = (4 * (5 * (lane >> 5) + (lane & 7)) + ((lane >> 3) & 3)).astype(F32)
    position = iota((384, 512), 0).astype(F32)
    results = []
    for layer in range(2):
        where = alt * 2 + layer
        shrink = 1.0 - bin_ref[where].astype(F32) * 0.03125
        weights = jnp.maximum(0.0, 1.0 - jnp.abs(position - column * shrink)).astype(BF16)
        rows = screen_ref[layer].astype(F32)
        parts = []
        for frame in range(2):
            for star in range(2):
                left = col_ref[frame, where, star]
                turned = pltpu.roll(rows, lax.rem(512 - left, 512), axis=1)
                parts.append(turned[:, :384])
        stacked = jnp.concatenate(parts, axis=0).astype(BF16)
        results.append(jnp.dot(stacked, weights, preferred_element_type=F32))
    group = iota((8, 128), 1) >> 5
    for star in range(2):
        for tile in range(4):
            slots = []
            for layer in range(2):
                for frame in range(2):
                    top = (frame * 2 + star) * 8
                    slots.append(results[layer][top : top + 8, tile * 128 : tile * 128 + 128])
            for inner in range(4):
                merged = jnp.zeros((8, 128), F32)
                for slot in range(4):
                    shift = (32 * (slot - inner)) % 128
                    moved = slots[slot] if shift == 0 else pltpu.roll(slots[slot], shift, axis=1)
                    merged = jnp.where(group == slot, moved, merged)
                out_ref[star * 16 + tile * 4 + inner] = merged


def rows_kernel(row_ref, bin_ref, got_ref, out_ref):
    star = lax.axis_index("xh")
    block = block_index()
    ring = lax.axis_index("zh") * 4 + lax.axis_index("zl")
    values = got_ref[...].reshape(256, 128)
    high = values.astype(BF16).astype(F32)
    low = values - high
    lane = iota((256, 128), 1)
    line = iota((256, 1), 0)
    z_to = line >> 4
    quarter = (line >> 2) & 3
    zl = z_to & 3
    first = (20 * zl - block + 15) >> 4
    pupil_row = (4 * (20 * quarter + 5 * (z_to >> 2) + first) + (line & 3)).astype(F32)
    cell = iota((1, 256), 1)
    owner = cell >> 5
    screen_row = ring * 32 + (cell & 31)
    sums = [jnp.zeros((256, 128), F32), jnp.zeros((256, 128), F32)]
    for layer in range(2):
        shrink = jnp.zeros((1, 256), F32)
        for alt in range(8):
            value = 1.0 - bin_ref[alt * 2 + layer].astype(F32) * 0.03125
            shrink = jnp.where(owner == alt, value, shrink)
        scaled = [pupil_row * shrink, (pupil_row + 4.0) * shrink]
        for frame in range(2):
            top = jnp.zeros((1, 256), I32)
            for alt in range(8):
                top = jnp.where(owner == alt, row_ref[frame, alt * 2 + layer, star], top)
            offset = (screen_row - top).astype(F32)
            slot = layer * 2 + frame
            shift = (64 * frame - 32 * slot) % 128
            moved = high if shift == 0 else pltpu.roll(high, shift, axis=1)
            shift = (64 * frame + 32 - 32 * slot) % 128
            other = low if shift == 0 else pltpu.roll(low, shift, axis=1)
            part = lane >> 5
            right = jnp.where(part == 2 * frame, moved, jnp.where(part == 2 * frame + 1, other, 0.0)).astype(BF16)
            for half in range(2):
                weights = jnp.maximum(0.0, 1.0 - jnp.abs(offset - scaled[half])).astype(BF16)
                sums[half] = sums[half] + jnp.dot(weights, right, preferred_element_type=F32)
    zero = sums[0] + pltpu.roll(sums[0], 96, axis=1)
    one = sums[1] + pltpu.roll(sums[1], 32, axis=1)
    out_ref[...] = jnp.where((lane & 63) < 32, zero, one).reshape(16, 16, 128)


def spread_kernel(got_ref, out_ref):
    total = jnp.sum(got_ref[...], axis=0)
    for quarter in range(4):
        top = (quarter // 2) * 8
        for ylc in range(4):
            out_ref[quarter * 4 + ylc] = total[top : top + 8]


def slopes_kernel(got_ref, light_ref, recon_ref, slopes_ref, out_ref, scratch):
    zl = lax.axis_index("zl")
    yh = lax.axis_index("yh")
    ylc = ylc_index()
    row = iota((8, 128), 0)
    lane = iota((8, 128), 1)
    cell = (lane & 63) >> 3
    phases = [jnp.zeros((8, 128), F32), jnp.zeros((8, 128), F32)]
    for i in range(5):
        flat = 20 * zl + 5 * ylc + i
        source = flat & 15
        slot = (flat >> 4) - ((20 * zl - source + 15) >> 4)
        block = got_ref[source]
        both = jnp.where((row >> 2) == yh, block, pltpu.roll(block, 4, axis=0))
        turned = []
        for q in range(4):
            shift = lax.rem(256 + 8 * i - 32 * slot - 8 * q, 128)
            turned.append(pltpu.roll(both, shift, axis=1))
        for h in range(2):
            pair = jnp.where(row < 4, turned[2 * h], turned[2 * h + 1])
            phases[h] = jnp.where(cell == i, pair, phases[h])
    scratch[...] = jnp.zeros((16, 128), F32)
    scratch[:, 0:25] = light_ref[...]
    wide = scratch[...]
    lane16 = iota((16, 128), 1)
    placed = jnp.ones((16, 128), F32)
    for frame in range(2):
        for i in range(5):
            shift = 64 * frame + 3 * i
            moved = wide if shift == 0 else pltpu.roll(wide, shift, axis=1)
            start = 64 * frame + 8 * i
            placed = jnp.where((lane16 >= start) & (lane16 < start + 5), moved, placed)
    scratch[...] = placed
    re, im = [], []
    for h in range(2):
        light = jnp.concatenate(
            [scratch[pl.ds(2 * h, 4, stride=4), :], scratch[pl.ds(2 * h + 1, 4, stride=4), :]], axis=0
        )
        re.append(light * jnp.cos(phases[h]))
        im.append(light * jnp.sin(phases[h]))
    power = re[0] * re[0] + im[0] * im[0] + re[1] * re[1] + im[1] * im[1]
    flux = jnp.sum(power, axis=0, keepdims=True)
    along_p = -4.0 * power
    pixel = row & 3
    for h in range(2):
        for d in range(1, 4):
            back_re = pltpu.roll(re[h], d, axis=0)
            back_im = pltpu.roll(im[h], d, axis=0)
            same = re[h] * back_re + im[h] * back_im
            cross = im[h] * back_re - re[h] * back_im
            sign = -8.0 if d % 2 == 0 else 8.0
            term = sign * same + (4.0 * LAG[d - 1]) * cross
            along_p = along_p + jnp.where(pixel >= d, term, 0.0)
    swap_re = [pltpu.roll(x, 4, axis=0) for x in re]
    swap_im = [pltpu.roll(x, 4, axis=0) for x in im]

    def term_of(to_re, to_im, from_re, from_im, d):
        same = to_re * from_re + to_im * from_im
        cross = to_im * from_re - to_re * from_im
        sign = -8.0 if d % 2 == 0 else 8.0
        return sign * same + (4.0 * LAG[d - 1]) * cross

    along_q = -4.0 * power
    upper = row >= 4
    for h in range(2):
        along_q = along_q + jnp.where(upper, term_of(re[h], im[h], swap_re[h], swap_im[h], 1), 0.0)
    along_q = along_q + term_of(re[1], im[1], re[0], im[0], 2)
    near = term_of(re[1], im[1], swap_re[0], swap_im[0], 1)
    far = term_of(re[1], im[1], swap_re[0], swap_im[0], 3)
    along_q = along_q + jnp.where(upper, far, near)
    scale = 0.125 / flux
    slope_p = jnp.sum(along_p, axis=0, keepdims=True) * scale
    slope_q = jnp.sum(along_q, axis=0, keepdims=True) * scale
    pair = jnp.where(row == 0, slope_p, slope_q)
    compact = []
    for frame in range(2):
        packed = jnp.zeros((8, 128), F32)
        for i in range(5):
            shift = (-64 * frame - 3 * i) % 128
            moved = pair if shift == 0 else pltpu.roll(pair, shift, axis=1)
            packed = jnp.where((lane >= 5 * i) & (lane < 5 * i + 5), moved, packed)
        compact.append(packed)
        slopes_ref[frame] = packed[0:2, 0:25]
    total = jnp.zeros((8, ACTUATORS), F32)
    for axis in range(2):
        left = jnp.where(row == 0, compact[0][axis : axis + 1], compact[1][axis : axis + 1])
        left = left[:, 0:25].astype(BF16)
        total = total + jnp.dot(left, recon_ref[axis], preferred_element_type=F32)
    for j in range(23):
        out_ref[j] = total[0:2, 256 * j : 256 * j + 256]
    out_ref[23] = jnp.zeros((2, 256), F32)
    out_ref[23, :, 0:112] = total[0:2, 5888:6000]
    for j in range(24, 32):
        out_ref[j] = jnp.zeros((2, 256), F32)


def sum_kernel(got_ref, out_ref):
    total = jnp.sum(got_ref[...], axis=0)
    for i in range(out_ref.shape[0]):
        out_ref[i] = total


def clip_kernel(got_ref, code_ref, out_ref):
    for j in range(24):
        width = 256 if j < 23 else 112
        update = got_ref[j][:, 0:width]
        limit = code_ref[:, 256 * j : 256 * j + width].astype(F32) * 0.125
        first = jnp.clip(0.5 * update[0:1], -limit, limit)
        second = jnp.clip(first + 0.5 * update[1:2], -limit, limit)
        out_ref[0:1, 256 * j : 256 * j + width] = first
        out_ref[1:2, 256 * j : 256 * j + width] = second


def call(body, outs, specs, *args, scratch=(), name=None):
    return pl.pallas_call(
        body,
        out_shape=outs,
        in_specs=specs,
        out_specs=jax.tree.map(lambda _: VMEM, outs),
        scratch_shapes=list(scratch),
        compiler_params=pltpu.CompilerParams(vmem_limit_bytes=16 * 1024 * 1024),
        name=name,
    )(*args)


def exchange(value, axes):
    return lax.all_to_all(value, axes, 0, 0, tiled=True)


def shards(screens, row_offset, col_offset, layer_bin, illumination, reconstructor, sat_code):
    shape = jax.ShapeDtypeStruct
    cols = call(columns_kernel, shape((32, 8, 128), F32), [SMEM, SMEM, VMEM], col_offset, layer_bin, screens, name="columns")
    cols = exchange(cols, PLANE)
    pupil = call(rows_kernel, shape((16, 16, 128), F32), [SMEM, SMEM, VMEM], row_offset, layer_bin, cols, name="rows")
    pupil = exchange(pupil, RING)
    owned = call(spread_kernel, shape((16, 8, 128), F32), [VMEM], pupil, name="spread")
    owned = exchange(owned, HALF)
    slopes, updates = call(
        slopes_kernel,
        (shape((2, 2, 25), F32), shape((32, 2, 256), F32)),
        [VMEM, VMEM, VMEM],
        owned,
        illumination,
        reconstructor,
        scratch=[pltpu.VMEM((16, 128), F32)],
        name="slopes",
    )
    updates = exchange(updates, PLANE)
    updates = call(sum_kernel, shape((16, 2, 256), F32), [VMEM], updates, name="sum_plane")
    updates = exchange(updates, RING)
    updates = call(sum_kernel, shape((32, 2, 256), F32), [VMEM], updates, name="sum_ring")
    updates = exchange(updates, PLANE)
    commands = call(
        clip_kernel, shape((2, ACTUATORS), F32), [VMEM, VMEM], updates, sat_code.reshape(1, ACTUATORS), name="clip"
    )
    return slopes, commands


def solution(mesh):
    fine = Mesh(mesh.devices.reshape(SIZES), NAMES)
    placed = (
        P(ALT, STRIP, None),
        P(),
        P(),
        P(),
        P(None, ALT + STRIP),
        P(None, ALT + STRIP, None),
        P(),
    )
    return jax.shard_map(
        shards,
        mesh=fine,
        in_specs=placed,
        out_specs=(P(None, None, ALT + STRIP), P()),
        check_vma=False,
    )
```

time: 636 us -> 103 us (0.16)
  waiting for transfers between devices: 477 us -> 20.9 us
  blocking collectives: 102 us -> 51 us
  starting transfers between devices: 0.04 us -> 22.4 us
  local copies, waits for them, and re-layouts: 20.2 us -> 0.99 us
  matrix products: 16.4 us -> 0 us
  between operations: 15.7 us -> 0.73 us
  Pallas kernels: 0 us -> 6.57 us
    unnamed x2 -> x0, waiting for transfers between devices: 477 us -> none
    psum x1 -> x0, blocking collectives: 102 us -> none  [shards(): updates = lax.psum(partial_value, ('alt', 'strip'))]
    all_to_all x0 -> x3, blocking collectives: none -> 51 us  [exchange(): return lax.all_to_all(value, axes, 0, 0, tiled=True)]
    all_to_all x0 -> x3, starting transfers between devices: none -> 22.4 us  [exchange(): return lax.all_to_all(value, axes, 0, 0, tiled=True)]
    all_to_all x0 -> x3, waiting for transfers between devices: none -> 20.9 us  [exchange(): return lax.all_to_all(value, axes, 0, 0, tiled=True)]
    dot_general x17 -> x0, matrix products: 16.4 us -> none  [the longest x4 4.92 us: shards(): jnp.einsum('dapr,drbq->pqdab', row_weights.reshape(GUIDE_STARS, LENSLETS,...]
    gather x24 -> x0, local copies, waits for them, and re-layouts: 10.4 us -> none
    pallas_call x0 -> x7, Pallas kernels: none -> 6.57 us  [call(): pl.pallas_call(body, out_shape=outs, in_specs=specs, out_specs=jax.tree.m...]
  transfers between devices with their start and end apart: 1 -> 3, of which waited for: 1 -> 3; matrix products, arithmetic and copies ran while one was open for 0% -> 0% of each run, Pallas kernels for 0% -> 0%
where the time goes in v1:
time: 103 us
  blocking collectives  51 us (50%)
  starting transfers between devices  22.4 us (22%)
  waiting for transfers between devices  20.9 us (20%)
  Pallas kernels  6.57 us (6%)
    all_to_all x3, blocking collectives, exchange(): return lax.all_to_all(value, axes, 0, 0, tiled=True)  51 us
    all_to_all x3, starting transfers between devices, exchange(): return lax.all_to_all(value, axes, 0, 0, tiled=True)  22.4 us
    all_to_all x3, waiting for transfers between devices, exchange(): return lax.all_to_all(value, axes, 0, 0, tiled=True)  20.9 us
    pallas_call x7, Pallas kernels, call(): pl.pallas_call(body, out_shape=outs, in_specs=specs, out_specs=jax.tree.m...  6.57 us
  transfers between devices with their start and end apart: 3, of which 3 were waited for; matrix products, arithmetic and copies ran while one was open for 0% of the time, Pallas kernels for 0%

profile of v1, /device:TPU:1, one launch (start us, length us, event | category | flops | bytes accessed | tf_op | source)
XLA Modules:
  0.0 102.7 jit_solution(7230379919262948108)
XLA Ops:
  0.6 0.0 copy-start.2
  0.6 0.0 copy-start
  0.6 0.8 copy.9.col_ref
  1.4 0.0 copy-done.2
  1.4 0.0 copy-done
  1.4 0.0 copy-start.5
  1.4 2.0 %columns.1 = f32[32,8,128]{2,1,0:T(8,128)} custom-call(s32[2,16,2]{2,1,0:T(8,128)S(1)} %copy.9.col_ref, s32[16]{0:T(128)S(1)} %copy-done.2, bf16[2,8,512]{2,1,0:T(8,128)(2,1)S(1)} %copy-done), custom_call_target="tpu_custom_call" | custom-call | tf_op jit(solution)/shard_map/columns/pallas_call | solution.py:246
  3.4 0.0 copy-start.3
  3.4 10.5 %all-to-all-start = ((f32[32,8,128]{2,1,0:T(8,128)}), f32[32,8,128]{2,1,0:T(8,128)S(1)}, u32[]{:S(2)}, u32[]{:S(2)}) async-start(f32[32,8,128]{2,1,0:T(8,128)} %columns.1), calls=%async_computation | async-start | bytes 262144 | tf_op jit(solution)/shard_map/all_to_all | solution.py:258
  13.9 0.0 copy-done.5
  13.9 0.1 copy.10.row_ref
  14.0 7.7 %all-to-all-done.got_ref = f32[32,8,128]{2,1,0:T(8,128)S(1)} async-done(((f32[32,8,128]{2,1,0:T(8,128)}), f32[32,8,128]{2,1,0:T(8,128)S(1)}, u32[]{:S(2)}, u32[]{:S(2)}) %all-to-all-start) | async-done | bytes 131104 | tf_op jit(solution)/shard_map/all_to_all | solution.py:258
  21.7 1.6 %rows.1 = f32[16,16,128]{2,1,0:T(8,128)S(1)} custom-call(s32[2,16,2]{2,1,0:T(8,128)S(1)} %copy.10.row_ref, s32[16]{0:T(128)S(1)} %copy-done.2, f32[32,8,128]{2,1,0:T(8,128)S(1)} %all-to-all-done.got_ref), custom_call_target="tpu_custom_call" | custom-call | tf_op jit(solution)/shard_map/rows/pallas_call | solution.py:246
  23.4 25.0 %all_to_all.30.got_ref = f32[16,16,128]{2,1,0:T(8,128)S(1)} all-to-all(f32[16,16,128]{2,1,0:T(8,128)S(1)} %rows.1), channel_id=1, replica_groups=mesh['xh'=2,'xl'=2,'yh'=2,'zh'=4,'zl'=4,'yl'=2,'co'=2] {'zh','zl'}, dimensions={0} | all-to-all | bytes 262144 | tf_op jit(solution)/shard_map/all_to_all | solution.py:258
  48.3 0.7 spread.1
  49.0 6.5 %all-to-all-start.2 = ((f32[16,8,128]{2,1,0:T(8,128)}), f32[16,8,128]{2,1,0:T(8,128)S(1)}, u32[]{:S(2)}, u32[]{:S(2)}) async-start(f32[16,8,128]{2,1,0:T(8,128)} %spread.1), calls=%async_computation.2 | async-start | bytes 131072 | tf_op jit(solution)/shard_map/all_to_all | solution.py:258
  55.5 0.0 copy-done.3
  55.5 0.0 copy-start.1
  55.5 0.1 copy.11.recon_ref
  55.6 5.8 %all-to-all-done.2.got_ref = f32[16,8,128]{2,1,0:T(8,128)S(1)} async-done(((f32[16,8,128]{2,1,0:T(8,128)}), f32[16,8,128]{2,1,0:T(8,128)S(1)}, u32[]{:S(2)}, u32[]{:S(2)}) %all-to-all-start.2) | async-done | bytes 65568 | tf_op jit(solution)/shard_map/all_to_all | solution.py:258
  61.4 0.0 copy-done.1
  61.4 0.9 slopes.1
  62.3 11.0 %all_to_all.31.got_ref = f32[32,2,256]{2,1,0:T(2,128)S(1)} all-to-all(f32[32,2,256]{2,1,0:T(2,128)S(1)} %get-tuple-element.5), channel_id=1, replica_groups=mesh['xh'=2,'xl'=2,'yh'=2,'zh'=4,'zl'=4,'yl'=2,'co'=2] {'xh','xl','yh','..., dimensions={0} | all-to-all | bytes 131072 | tf_op jit(solution)/shard_map/all_to_all | solution.py:258
  73.3 15.1 %all_to_all.32.got_ref = f32[16,2,256]{2,1,0:T(2,128)S(1)} all-to-all(f32[16,2,256]{2,1,0:T(2,128)S(1)} %sum_plane.1), channel_id=1, replica_groups=mesh['xh'=2,'xl'=2,'yh'=2,'zh'=4,'zl'=4,'yl'=2,'co'=2] {'zh','zl'}, dimensions={0} | all-to-all | bytes 65536 | tf_op jit(solution)/shard_map/all_to_all | solution.py:258
  88.5 0.7 sum_ring.1
  89.1 0.0 copy-start.4
  89.1 5.4 %all-to-all-start.5 = ((f32[32,2,256]{2,1,0:T(2,128)}), f32[32,2,256]{2,1,0:T(2,128)S(1)}, u32[]{:S(2)}, u32[]{:S(2)}) async-start(f32[32,2,256]{2,1,0:T(2,128)} %sum_ring.1), calls=%async_computation.5 | async-start | bytes 131072 | tf_op jit(solution)/shard_map/all_to_all | solution.py:258
  94.5 0.0 copy-done.4
  94.5 7.4 %all-to-all-done.5.got_ref = f32[32,2,256]{2,1,0:T(2,128)S(1)} async-done(((f32[32,2,256]{2,1,0:T(2,128)}), f32[32,2,256]{2,1,0:T(2,128)S(1)}, u32[]{:S(2)}, u32[]{:S(2)}) %all-to-all-start.5) | async-done | bytes 65568 | tf_op jit(solution)/shard_map/all_to_all | solution.py:258
  102.0 0.7 clip.1
  (2 shorter events, 0.1 us)
Async XLA Ops:
  0.6 0.8 copy-start.2
  0.6 0.8 copy-start
  1.4 12.5 %copy-start.5 = (s32[2,16,2]{1,2,0:T(2,128)S(1)}, s32[2,16,2]{1,2,0:T(2,128)}, u32[]{:S(2)}) copy-start(s32[2,16,2]{1,2,0:T(2,128)} %param.8) | copy-start | bytes 772
  3.4 52.1 %copy-start.3 = (bf16[2,25,6000]{2,0,1:T(2,128)(2,1)S(1)}, bf16[2,25,6000]{2,0,1:T(2,128)(2,1)}, u32[]{:S(2)}) copy-start(bf16[2,25,6000]{2,0,1:T(2,128)(2,1)} %param.12) | copy-start | bytes 1800004
  3.4 18.3 %all-to-all-start = ((f32[32,8,128]{2,1,0:T(8,128)}), f32[32,8,128]{2,1,0:T(8,128)S(1)}, u32[]{:S(2)}, u32[]{:S(2)}) async-start(f32[32,8,128]{2,1,0:T(8,128)} %columns.1), calls=%async_computation | async-start | bytes 262144 | tf_op jit(solution)/shard_map/all_to_all | solution.py:258
  49.0 12.4 %all-to-all-start.2 = ((f32[16,8,128]{2,1,0:T(8,128)}), f32[16,8,128]{2,1,0:T(8,128)S(1)}, u32[]{:S(2)}, u32[]{:S(2)}) async-start(f32[16,8,128]{2,1,0:T(8,128)} %spread.1), calls=%async_computation.2 | async-start | bytes 131072 | tf_op jit(solution)/shard_map/all_to_all | solution.py:258
  55.5 5.9 %copy-start.1 = (f32[16,25]{1,0:T(8,128)S(1)}, f32[16,25]{1,0:T(8,128)}, u32[]{:S(2)}) copy-start(f32[16,25]{1,0:T(8,128)} %light_ref.1) | copy-start | bytes 4804
  89.1 5.4 %copy-start.4 = (s32[6000]{0:T(1024)S(1)}, s32[6000]{0:T(1024)}, u32[]{:S(2)}) copy-start(s32[6000]{0:T(1024)} %param.13) | copy-start | bytes 72004
  89.1 12.9 %all-to-all-start.5 = ((f32[32,2,256]{2,1,0:T(2,128)}), f32[32,2,256]{2,1,0:T(2,128)S(1)}, u32[]{:S(2)}, u32[]{:S(2)}) async-start(f32[32,2,256]{2,1,0:T(2,128)} %sum_ring.1), calls=%async_computation.5 | async-start | bytes 131072 | tf_op jit(solution)/shard_map/all_to_all | solution.py:258

commit v2 on v1

--- a/solution.py
+++ b/solution.py
@@ -44,7 +44,10 @@
 def columns_kernel(col_ref, bin_ref, screen_ref, out_ref):
     alt = alt_index()
     lane = iota((1, 512), 1)
-    column = (4 * (5 * (lane >> 5) + (lane & 7)) + ((lane >> 3) & 3)).astype(F32)
+    block = lane >> 5
+    part = (lane & 31) >> 2
+    lenslet = jnp.where(part < 4, 20 * part + block, 20 * (block >> 2) + 16 + (block & 3))
+    column = (4 * lenslet + (lane & 3)).astype(F32)
     position = iota((384, 512), 0).astype(F32)
     results = []
     for layer in range(2):
@@ -77,96 +80,99 @@
                 out_ref[star * 16 + tile * 4 + inner] = merged
 
 
-def rows_kernel(row_ref, bin_ref, got_ref, out_ref):
+def rows_kernel(row_ref, bin_ref, light_ref, got_ref, out_ref, light_out, scratch):
     star = lax.axis_index("xh")
     block = block_index()
     ring = lax.axis_index("zh") * 4 + lax.axis_index("zl")
     values = got_ref[...].reshape(256, 128)
     high = values.astype(BF16).astype(F32)
     low = values - high
-    lane = iota((256, 128), 1)
-    line = iota((256, 1), 0)
-    z_to = line >> 4
-    quarter = (line >> 2) & 3
-    zl = z_to & 3
-    first = (20 * zl - block + 15) >> 4
-    pupil_row = (4 * (20 * quarter + 5 * (z_to >> 2) + first) + (line & 3)).astype(F32)
+    wide = iota((256, 128), 1)
+    rights = [
+        jnp.where(wide < 64, high, pltpu.roll(low, 64, axis=1)).astype(BF16),
+        jnp.where(wide < 64, pltpu.roll(high, 64, axis=1), low).astype(BF16),
+    ]
+    line = iota((64, 1), 0)
+    base = (80 * ((line >> 2) & 3) + 20 * (line >> 4) + (line & 3)).astype(F32)
+    pupil_row = jnp.concatenate([base + 4.0 * rr for rr in range(5)], axis=0)
     cell = iota((1, 256), 1)
     owner = cell >> 5
     screen_row = ring * 32 + (cell & 31)
-    sums = [jnp.zeros((256, 128), F32), jnp.zeros((256, 128), F32)]
+    sums = [None, None]
     for layer in range(2):
         shrink = jnp.zeros((1, 256), F32)
         for alt in range(8):
             value = 1.0 - bin_ref[alt * 2 + layer].astype(F32) * 0.03125
             shrink = jnp.where(owner == alt, value, shrink)
-        scaled = [pupil_row * shrink, (pupil_row + 4.0) * shrink]
+        scaled = pupil_row * shrink
         for frame in range(2):
             top = jnp.zeros((1, 256), I32)
             for alt in range(8):
-                top = jnp.where(owner == alt, row_ref[frame, alt * 2 + layer, star], top)
+                top = jnp.where(owner == alt, row_ref[frame, star, alt * 2 + layer], top)
             offset = (screen_row - top).astype(F32)
-            slot = layer * 2 + frame
-            shift = (64 * frame - 32 * slot) % 128
-            moved = high if shift == 0 else pltpu.roll(high, shift, axis=1)
-            shift = (64 * frame + 32 - 32 * slot) % 128
-            other = low if shift == 0 else pltpu.roll(low, shift, axis=1)
-            part = lane >> 5
-            right = jnp.where(part == 2 * frame, moved, jnp.where(part == 2 * frame + 1, other, 0.0)).astype(BF16)
-            for half in range(2):
-                weights = jnp.maximum(0.0, 1.0 - jnp.abs(offset - scaled[half])).astype(BF16)
-                sums[half] = sums[half] + jnp.dot(weights, right, preferred_element_type=F32)
-    zero = sums[0] + pltpu.roll(sums[0], 96, axis=1)
-    one = sums[1] + pltpu.roll(sums[1], 32, axis=1)
-    out_ref[...] = jnp.where((lane & 63) < 32, zero, one).reshape(16, 16, 128)
-
-
-def spread_kernel(got_ref, out_ref):
-    total = jnp.sum(got_ref[...], axis=0)
-    for quarter in range(4):
-        top = (quarter // 2) * 8
-        for ylc in range(4):
-            out_ref[quarter * 4 + ylc] = total[top : top + 8]
+            weights = jnp.maximum(0.0, 1.0 - jnp.abs(offset - scaled)).astype(BF16)
+            term = jnp.dot(weights, rights[layer], preferred_element_type=F32)
+            sums[frame] = term if layer == 0 else sums[frame] + term
+    lane = iota((8, 128), 1)
+    cell = lane & 31
+    odd = (lane & 32) != 0
+    kind = jnp.where(cell < 16, cell >> 2, block >> 2)
+    for t in range(4):
+        pieces = []
+        for rr in range(5):
+            halves = []
+            for h in range(2):
+                start = rr * 64 + t * 16 + h * 8
+                both = jnp.where(odd, sums[1][start : start + 8], sums[0][start : start + 8])
+                halves.append(both + pltpu.roll(both, 64, axis=1))
+            pieces.append(jnp.where(lane < 64, halves[0], halves[1]))
+        for zl in range(4):
+            here, after = pieces[zl], pieces[zl + 1]
+            first = jnp.where(kind < zl, after, here)
+            second = jnp.where(cell < 24, pltpu.roll(after, 20 - 4 * zl, axis=1), pltpu.roll(after, 8, axis=1))
+            out_ref[t * 4 + zl] = jnp.where(cell < 20, first, second)
+    scratch[...] = jnp.ones((16, 128), F32)
+    scratch[:, 0:25] = light_ref[...]
+    wide = scratch[...]
+    inside = iota((16, 128), 1)
+    scratch[...] = jnp.where((inside >= 32) & (inside < 57), pltpu.roll(wide, 32, axis=1), wide)
+    for q in range(4):
+        top = (q % 2) * 4
+        light_out[q // 2, top : top + 4, :] = scratch[pl.ds(q, 4, stride=4), :]
 
 
 def slopes_kernel(got_ref, light_ref, recon_ref, slopes_ref, out_ref, scratch):
+    xl = lax.axis_index("xl")
+    yh = lax.axis_index("yh")
     zl = lax.axis_index("zl")
-    yh = lax.axis_index("yh")
-    ylc = ylc_index()
     row = iota((8, 128), 0)
     lane = iota((8, 128), 1)
-    cell = (lane & 63) >> 3
+    mine = (row >> 2) == yh
+    for source in range(16):
+        block = got_ref[source]
+        block = jnp.where(xl == 0, block, pltpu.roll(block, 64, axis=1))
+        scratch[source] = jnp.where(mine, block, pltpu.roll(block, 4, axis=0))
+    cell = lane & 31
     phases = [jnp.zeros((8, 128), F32), jnp.zeros((8, 128), F32)]
-    for i in range(5):
-        flat = 20 * zl + 5 * ylc + i
-        source = flat & 15
-        slot = (flat >> 4) - ((20 * zl - source + 15) >> 4)
-        block = got_ref[source]
-        both = jnp.where((row >> 2) == yh, block, pltpu.roll(block, 4, axis=0))
-        turned = []
-        for q in range(4):
-            shift = lax.rem(256 + 8 * i - 32 * slot - 8 * q, 128)
-            turned.append(pltpu.roll(both, shift, axis=1))
+    flat_start = 100 * zl + 25 * ylc_index()
+    for n in range(25):
+        flat = flat_start + n
+        lens_row = (flat * 205) >> 14
+        lens_col = flat - 80 * lens_row
+        kind = (lens_col * 205) >> 12
+        index = lens_col - 20 * kind
+        regular = index < 16
+        source = jnp.where(regular, index, 4 * kind + index - 16)
+        first = lens_row == zl + (kind < zl).astype(I32)
+        place = jnp.where(regular, jnp.where(first, 4 * kind, 20), jnp.where(first, 16, 24))
+        block = scratch[source]
+        turned = [pltpu.roll(block, (n + 128 - q - place) & 127, axis=1) for q in range(4)]
         for h in range(2):
             pair = jnp.where(row < 4, turned[2 * h], turned[2 * h + 1])
-            phases[h] = jnp.where(cell == i, pair, phases[h])
-    scratch[...] = jnp.zeros((16, 128), F32)
-    scratch[:, 0:25] = light_ref[...]
-    wide = scratch[...]
-    lane16 = iota((16, 128), 1)
-    placed = jnp.ones((16, 128), F32)
-    for frame in range(2):
-        for i in range(5):
-            shift = 64 * frame + 3 * i
-            moved = wide if shift == 0 else pltpu.roll(wide, shift, axis=1)
-            start = 64 * frame + 8 * i
-            placed = jnp.where((lane16 >= start) & (lane16 < start + 5), moved, placed)
-    scratch[...] = placed
+            phases[h] = jnp.where(cell == n, pair, phases[h])
     re, im = [], []
     for h in range(2):
-        light = jnp.concatenate(
-            [scratch[pl.ds(2 * h, 4, stride=4), :], scratch[pl.ds(2 * h + 1, 4, stride=4), :]], axis=0
-        )
+        light = light_ref[h]
         re.append(light * jnp.cos(phases[h]))
         im.append(light * jnp.sin(phases[h]))
     power = re[0] * re[0] + im[0] * im[0] + re[1] * re[1] + im[1] * im[1]
@@ -203,15 +209,9 @@
     slope_p = jnp.sum(along_p, axis=0, keepdims=True) * scale
     slope_q = jnp.sum(along_q, axis=0, keepdims=True) * scale
     pair = jnp.where(row == 0, slope_p, slope_q)
-    compact = []
+    compact = [pair, pltpu.roll(pair, 96, axis=1)]
     for frame in range(2):
-        packed = jnp.zeros((8, 128), F32)
-        for i in range(5):
-            shift = (-64 * frame - 3 * i) % 128
-            moved = pair if shift == 0 else pltpu.roll(pair, shift, axis=1)
-            packed = jnp.where((lane >= 5 * i) & (lane < 5 * i + 5), moved, packed)
-        compact.append(packed)
-        slopes_ref[frame] = packed[0:2, 0:25]
+        slopes_ref[frame] = compact[frame]
     total = jnp.zeros((8, ACTUATORS), F32)
     for axis in range(2):
         left = jnp.where(row == 0, compact[0][axis : axis + 1], compact[1][axis : axis + 1])
@@ -231,11 +231,12 @@
         out_ref[i] = total
 
 
-def clip_kernel(got_ref, code_ref, out_ref):
+def clip_kernel(got_ref, code_ref, slopes_ref, slopes_out, out_ref):
+    slopes_out[...] = slopes_ref[:, 0:2, 0:25]
     for j in range(24):
         width = 256 if j < 23 else 112
         update = got_ref[j][:, 0:width]
-        limit = code_ref[:, 256 * j : 256 * j + width].astype(F32) * 0.125
+        limit = code_ref[256 * j : 256 * j + width].reshape(1, width).astype(F32) * 0.125
         first = jnp.clip(0.5 * update[0:1], -limit, limit)
         second = jnp.clip(first + 0.5 * update[1:2], -limit, limit)
         out_ref[0:1, 256 * j : 256 * j + width] = first
@@ -260,20 +261,32 @@
 
 def shards(screens, row_offset, col_offset, layer_bin, illumination, reconstructor, sat_code):
     shape = jax.ShapeDtypeStruct
+    row_offset = jnp.transpose(row_offset, (0, 2, 1))
     cols = call(columns_kernel, shape((32, 8, 128), F32), [SMEM, SMEM, VMEM], col_offset, layer_bin, screens, name="columns")
     cols = exchange(cols, PLANE)
-    pupil = call(rows_kernel, shape((16, 16, 128), F32), [SMEM, SMEM, VMEM], row_offset, layer_bin, cols, name="rows")
+    pupil, light = call(
+        rows_kernel,
+        (shape((16, 8, 128), F32), shape((2, 8, 128), F32)),
+        [SMEM, SMEM, VMEM, VMEM],
+        row_offset,
+        layer_bin,
+        illumination,
+        cols,
+        scratch=[pltpu.VMEM((16, 128), F32)],
+        name="rows",
+    )
     pupil = exchange(pupil, RING)
-    owned = call(spread_kernel, shape((16, 8, 128), F32), [VMEM], pupil, name="spread")
+    owned = call(sum_kernel, shape((16, 8, 128), F32), [VMEM], pupil, name="spread")
     owned = exchange(owned, HALF)
+    owned, reconstructor = lax.optimization_barrier((owned, reconstructor))
     slopes, updates = call(
         slopes_kernel,
-        (shape((2, 2, 25), F32), shape((32, 2, 256), F32)),
+        (shape((2, 8, 128), F32), shape((32, 2, 256), F32)),
         [VMEM, VMEM, VMEM],
         owned,
-        illumination,
+        light,
         reconstructor,
-        scratch=[pltpu.VMEM((16, 128), F32)],
+        scratch=[pltpu.VMEM((16, 8, 128), F32)],
         name="slopes",
     )
     updates = exchange(updates, PLANE)
@@ -281,10 +294,15 @@
     updates = exchange(updates, RING)
     updates = call(sum_kernel, shape((32, 2, 256), F32), [VMEM], updates, name="sum_ring")
     updates = exchange(updates, PLANE)
-    commands = call(
-        clip_kernel, shape((2, ACTUATORS), F32), [VMEM, VMEM], updates, sat_code.reshape(1, ACTUATORS), name="clip"
-    )
-    return slopes, commands
+    return call(
+        clip_kernel,
+        (shape((2, 2, 25), F32), shape((2, ACTUATORS), F32)),
+        [VMEM, VMEM, VMEM],
+        updates,
+        sat_code,
+        slopes,
+        name="clip",
+    )
 
 
 def solution(mesh):

time: 103 us -> 96.8 us (0.940)
  blocking collectives: 51 us -> 90.8 us
  starting transfers between devices: 22.4 us -> 0 us
  waiting for transfers between devices: 20.9 us -> 0 us
  Pallas kernels: 6.57 us -> 3.95 us
    all_to_all x3 -> x6, blocking collectives: 51 us -> 90.8 us  [exchange(): return lax.all_to_all(value, axes, 0, 0, tiled=True)]
    all_to_all x3 -> x0, starting transfers between devices: 22.4 us -> none  [exchange(): return lax.all_to_all(value, axes, 0, 0, tiled=True)]
    all_to_all x3 -> x0, waiting for transfers between devices: 20.9 us -> none  [exchange(): return lax.all_to_all(value, axes, 0, 0, tiled=True)]
    pallas_call x7, Pallas kernels: 6.57 us -> 3.95 us  [call(): pl.pallas_call(body, out_shape=outs, in_specs=specs, out_specs=jax.tree.m...]
  transfers between devices with their start and end apart: 3 -> 0, of which waited for: 3 -> 0; matrix products, arithmetic and copies ran while one was open for 0% -> 0% of each run, Pallas kernels for 0% -> 0%
where the time goes in v2:
time: 96.8 us; the launch traced here: 96.3 us
  blocking collectives  90.8 us (94%)
  Pallas kernels  3.95 us (4%)
    all_to_all x6, blocking collectives, exchange(): return lax.all_to_all(value, axes, 0, 0, tiled=True)  90.8 us
    pallas_call x7, Pallas kernels, call(): pl.pallas_call(body, out_shape=outs, in_specs=specs, out_specs=jax.tree.m...  3.95 us

profile of v2, /device:TPU:1, one launch (start us, length us, event | category | flops | bytes accessed | tf_op | source)
XLA Modules:
  0.0 96.3 jit_solution(15635425055341448267)
XLA Ops:
  0.6 0.0 copy-start.4
  0.6 0.0 copy-start.1
  0.6 0.8 copy.9.col_ref
  1.4 0.0 copy-done.4
  1.4 0.0 copy-done.1
  1.4 1.3 %columns.1 = f32[32,8,128]{2,1,0:T(8,128)S(1)} custom-call(s32[2,16,2]{2,1,0:T(8,128)S(1)} %copy.9.col_ref, s32[16]{0:T(128)S(1)} %copy-done.4, bf16[2,8,512]{2,1,0:T(8,128)(2,1)S(1)} %copy-done.1), custom_call_target="tpu_custom_call" | custom-call | tf_op jit(solution)/shard_map/columns/pallas_call | solution.py:247
  2.8 0.0 copy-start.2
  2.8 0.0 copy-start.3
  2.8 0.0 copy-start.5
  2.8 17.5 %all_to_all.30.got_ref = f32[32,8,128]{2,1,0:T(8,128)S(1)} all-to-all(f32[32,8,128]{2,1,0:T(8,128)S(1)} %columns.1), channel_id=1, replica_groups=mesh['xh'=2,'xl'=2,'yh'=2,'zh'=4,'zl'=4,'yl'=2,'co'=2] {'xh','xl','yh','..., dimensions={0} | all-to-all | bytes 262144 | tf_op jit(solution)/shard_map/all_to_all | solution.py:259
  20.2 0.0 copy-done.2
  20.2 0.0 copy-done.3
  20.3 1.2 %rows.1 = (f32[16,8,128]{2,1,0:T(8,128)S(1)}, f32[2,8,128]{2,1,0:T(8,128)S(1)}) custom-call(s32[2,2,16]{2,1,0:T(2,128)S(1)} %bitcast.1, s32[16]{0:T(128)S(1)} %copy-done.4, f32[16,25]{1,0:T(8,128)S(1)} %copy-done.2, f32[32,8,128]{2,1,0:T(8,128)S(1)} %all_to_all.30.got_ref), custom_call_target="tpu_custom_call" | custom-call | tf_op jit(solution)/shard_map/rows/pallas_call | solution.py:247
  21.4 25.1 %all_to_all.31.got_ref = f32[16,8,128]{2,1,0:T(8,128)S(1)} all-to-all(f32[16,8,128]{2,1,0:T(8,128)S(1)} %get-tuple-element.8), channel_id=1, replica_groups=mesh['xh'=2,'xl'=2,'yh'=2,'zh'=4,'zl'=4,'yl'=2,'co'=2] {'zh','zl'}, dimensions={0} | all-to-all | bytes 131072 | tf_op jit(solution)/shard_map/all_to_all | solution.py:259
  46.5 10.4 %all_to_all.32.got_ref = f32[16,8,128]{2,1,0:T(8,128)S(1)} all-to-all(f32[16,8,128]{2,1,0:T(8,128)S(1)} %spread.1), channel_id=1, replica_groups=mesh['xh'=2,'xl'=2,'yh'=2,'zh'=4,'zl'=4,'yl'=2,'co'=2] {'xl','yh','yl','..., dimensions={0} | all-to-all | bytes 131072 | tf_op jit(solution)/shard_map/all_to_all | solution.py:259
  56.9 0.0 copy-done.5
  56.9 0.1 copy.10.recon_ref
  57.0 0.7 slopes.1
  57.7 11.6 %all_to_all.33.got_ref = f32[32,2,256]{2,1,0:T(2,128)S(1)} all-to-all(f32[32,2,256]{2,1,0:T(2,128)S(1)} %get-tuple-element.12), channel_id=1, replica_groups=mesh['xh'=2,'xl'=2,'yh'=2,'zh'=4,'zl'=4,'yl'=2,'co'=2] {'xh','xl','yh','..., dimensions={0} | all-to-all | bytes 131072 | tf_op jit(solution)/shard_map/all_to_all | solution.py:259
  69.4 14.0 %all_to_all.34.got_ref = f32[16,2,256]{2,1,0:T(2,128)S(1)} all-to-all(f32[16,2,256]{2,1,0:T(2,128)S(1)} %sum_plane.1), channel_id=1, replica_groups=mesh['xh'=2,'xl'=2,'yh'=2,'zh'=4,'zl'=4,'yl'=2,'co'=2] {'zh','zl'}, dimensions={0} | all-to-all | bytes 65536 | tf_op jit(solution)/shard_map/all_to_all | solution.py:259
  83.4 0.0 copy-start
  83.4 12.3 %all_to_all.35.got_ref = f32[32,2,256]{2,1,0:T(2,128)S(1)} all-to-all(f32[32,2,256]{2,1,0:T(2,128)S(1)} %sum_ring.1), channel_id=1, replica_groups=mesh['xh'=2,'xl'=2,'yh'=2,'zh'=4,'zl'=4,'yl'=2,'co'=2] {'xh','xl','yh','..., dimensions={0} | all-to-all | bytes 131072 | tf_op jit(solution)/shard_map/all_to_all | solution.py:259
  95.7 0.0 copy-done
  95.7 0.7 clip.1
  (3 shorter events, 0.1 us)
Async XLA Ops:
  0.6 0.8 copy-start.4
  0.6 0.8 copy-start.1
  2.8 17.5 %copy-start.2 = (f32[16,25]{1,0:T(8,128)S(1)}, f32[16,25]{1,0:T(8,128)}, u32[]{:S(2)}) copy-start(f32[16,25]{1,0:T(8,128)} %light_ref.1) | copy-start | bytes 4804
  2.8 17.5 %copy-start.3 = (s32[2,16,2]{1,2,0:T(2,128)S(1)}, s32[2,16,2]{1,2,0:T(2,128)}, u32[]{:S(2)}) copy-start(s32[2,16,2]{1,2,0:T(2,128)} %param.8) | copy-start | bytes 772
  2.8 54.1 %copy-start.5 = (bf16[2,25,6000]{2,0,1:T(2,128)(2,1)S(1)}, bf16[2,25,6000]{2,0,1:T(2,128)(2,1)}, u32[]{:S(2)}) copy-start(bf16[2,25,6000]{2,0,1:T(2,128)(2,1)} %param.12) | copy-start | bytes 1800004
  83.4 12.3 %copy-start = (s32[6000]{0:T(1024)S(1)}, s32[6000]{0:T(1024)}, u32[]{:S(2)}) copy-start(s32[6000]{0:T(1024)} %code_ref.1) | copy-start | bytes 72004

commit v3 on v2

--- a/solution.py
+++ b/solution.py
@@ -21,7 +21,6 @@
 ROOT = 2.0**0.5
 LAG = (2.0 + 2.0 * ROOT, -2.0, 2.0 * ROOT - 2.0)
 
-SMEM = pl.BlockSpec(memory_space=pltpu.SMEM)
 VMEM = pl.BlockSpec(memory_space=pltpu.VMEM)
 
 
@@ -50,16 +49,17 @@
     column = (4 * lenslet + (lane & 3)).astype(F32)
     position = iota((384, 512), 0).astype(F32)
     results = []
+    bins = bin_ref[...].reshape(1, 16)
+    lefts = [col_ref[frame, pl.ds(2 * alt, 2), :] for frame in range(2)]
     for layer in range(2):
-        where = alt * 2 + layer
-        shrink = 1.0 - bin_ref[where].astype(F32) * 0.03125
+        chosen = jnp.where(iota((1, 16), 1) == 2 * alt + layer, bins, 0).astype(F32)
+        shrink = 1.0 - jnp.sum(chosen, axis=1, keepdims=True) * 0.03125
         weights = jnp.maximum(0.0, 1.0 - jnp.abs(position - column * shrink)).astype(BF16)
         rows = screen_ref[layer].astype(F32)
         parts = []
         for frame in range(2):
             for star in range(2):
-                left = col_ref[frame, where, star]
-                turned = pltpu.roll(rows, lax.rem(512 - left, 512), axis=1)
+                turned = pltpu.roll(rows, (512 - lefts[frame][layer, star]) & 511, axis=1)
                 parts.append(turned[:, :384])
         stacked = jnp.concatenate(parts, axis=0).astype(BF16)
         results.append(jnp.dot(stacked, weights, preferred_element_type=F32))
@@ -95,21 +95,21 @@
     line = iota((64, 1), 0)
     base = (80 * ((line >> 2) & 3) + 20 * (line >> 4) + (line & 3)).astype(F32)
     pupil_row = jnp.concatenate([base + 4.0 * rr for rr in range(5)], axis=0)
-    cell = iota((1, 256), 1)
-    owner = cell >> 5
-    screen_row = ring * 32 + (cell & 31)
+    screen_row = (ring * 32 + (iota((1, 256), 1) & 31)).astype(F32)
+    tops = [jnp.where(star == 0, row_ref[frame, 0:1, :], row_ref[frame, 1:2, :]) for frame in range(2)]
+    parts = [top >> 4 for top in tops] + [top & 15 for top in tops] + [bin_ref[...].reshape(1, 16)]
+    line16 = iota((8, 16), 0)
+    packed = jnp.zeros((8, 16), F32)
+    for n, part in enumerate(parts):
+        packed = jnp.where(line16 == n, part.astype(F32), packed)
+    packed = packed.astype(BF16)
     sums = [None, None]
     for layer in range(2):
-        shrink = jnp.zeros((1, 256), F32)
-        for alt in range(8):
-            value = 1.0 - bin_ref[alt * 2 + layer].astype(F32) * 0.03125
-            shrink = jnp.where(owner == alt, value, shrink)
-        scaled = pupil_row * shrink
+        pick = (iota((16, 256), 0) == 2 * (iota((16, 256), 1) >> 5) + layer).astype(F32).astype(BF16)
+        lanes = jnp.dot(packed, pick, preferred_element_type=F32)
+        scaled = pupil_row * (1.0 - lanes[4:5] * 0.03125)
         for frame in range(2):
-            top = jnp.zeros((1, 256), I32)
-            for alt in range(8):
-                top = jnp.where(owner == alt, row_ref[frame, star, alt * 2 + layer], top)
-            offset = (screen_row - top).astype(F32)
+            offset = screen_row - (16.0 * lanes[frame : frame + 1] + lanes[2 + frame : 3 + frame])
             weights = jnp.maximum(0.0, 1.0 - jnp.abs(offset - scaled)).astype(BF16)
             term = jnp.dot(weights, rights[layer], preferred_element_type=F32)
             sums[frame] = term if layer == 0 else sums[frame] + term
@@ -141,17 +141,19 @@
         light_out[q // 2, top : top + 4, :] = scratch[pl.ds(q, 4, stride=4), :]
 
 
-def slopes_kernel(got_ref, light_ref, recon_ref, slopes_ref, out_ref, scratch):
-    xl = lax.axis_index("xl")
-    yh = lax.axis_index("yh")
+def spread_kernel(got_ref, out_ref):
+    total = jnp.sum(got_ref[...], axis=0)
+    turned = [total, pltpu.roll(total, 64, axis=1)]
+    for quarter in range(4):
+        piece = turned[quarter // 2][(quarter % 2) * 4 : (quarter % 2) * 4 + 4]
+        for ylc in range(4):
+            out_ref[quarter * 4 + ylc] = piece
+
+
+def slopes_kernel(got_ref, light_ref, recon_ref, slopes_ref, out_ref):
     zl = lax.axis_index("zl")
     row = iota((8, 128), 0)
     lane = iota((8, 128), 1)
-    mine = (row >> 2) == yh
-    for source in range(16):
-        block = got_ref[source]
-        block = jnp.where(xl == 0, block, pltpu.roll(block, 64, axis=1))
-        scratch[source] = jnp.where(mine, block, pltpu.roll(block, 4, axis=0))
     cell = lane & 31
     phases = [jnp.zeros((8, 128), F32), jnp.zeros((8, 128), F32)]
     flat_start = 100 * zl + 25 * ylc_index()
@@ -165,7 +167,8 @@
         source = jnp.where(regular, index, 4 * kind + index - 16)
         first = lens_row == zl + (kind < zl).astype(I32)
         place = jnp.where(regular, jnp.where(first, 4 * kind, 20), jnp.where(first, 16, 24))
-        block = scratch[source]
+        block = got_ref[source]
+        block = jnp.concatenate([block, block], axis=0)
         turned = [pltpu.roll(block, (n + 128 - q - place) & 127, axis=1) for q in range(4)]
         for h in range(2):
             pair = jnp.where(row < 4, turned[2 * h], turned[2 * h + 1])
@@ -262,12 +265,12 @@
 def shards(screens, row_offset, col_offset, layer_bin, illumination, reconstructor, sat_code):
     shape = jax.ShapeDtypeStruct
     row_offset = jnp.transpose(row_offset, (0, 2, 1))
-    cols = call(columns_kernel, shape((32, 8, 128), F32), [SMEM, SMEM, VMEM], col_offset, layer_bin, screens, name="columns")
+    cols = call(columns_kernel, shape((32, 8, 128), F32), [VMEM, VMEM, VMEM], col_offset, layer_bin, screens, name="columns")
     cols = exchange(cols, PLANE)
     pupil, light = call(
         rows_kernel,
         (shape((16, 8, 128), F32), shape((2, 8, 128), F32)),
-        [SMEM, SMEM, VMEM, VMEM],
+        [VMEM, VMEM, VMEM, VMEM],
         row_offset,
         layer_bin,
         illumination,
@@ -276,7 +279,7 @@
         name="rows",
     )
     pupil = exchange(pupil, RING)
-    owned = call(sum_kernel, shape((16, 8, 128), F32), [VMEM], pupil, name="spread")
+    owned = call(spread_kernel, shape((16, 4, 128), F32), [VMEM], pupil, name="spread")
     owned = exchange(owned, HALF)
     owned, reconstructor = lax.optimization_barrier((owned, reconstructor))
     slopes, updates = call(
@@ -286,7 +289,6 @@
         owned,
         light,
         reconstructor,
-        scratch=[pltpu.VMEM((16, 8, 128), F32)],
         name="slopes",
     )
     updates = exchange(updates, PLANE)

time: 96.8 us -> 95.5 us (0.987)
  Pallas kernels: 3.95 us -> 2.78 us
    pallas_call x7, Pallas kernels: 3.95 us -> 2.78 us  [call(): pl.pallas_call(body, out_shape=outs, in_specs=specs, out_specs=jax.tree.m...]
where the time goes in v3:
time: 95.5 us; the launch traced here: 95.1 us
  blocking collectives  90.7 us (95%)
  Pallas kernels  2.78 us (3%)
    all_to_all x6, blocking collectives, exchange(): return lax.all_to_all(value, axes, 0, 0, tiled=True)  90.7 us
    pallas_call x7, Pallas kernels, call(): pl.pallas_call(body, out_shape=outs, in_specs=specs, out_specs=jax.tree.m...  2.78 us

profile of v3, /device:TPU:1, one launch (start us, length us, event | category | flops | bytes accessed | tf_op | source)
XLA Modules:
  0.0 95.1 jit_solution(8460047458855013640)
XLA Ops:
  0.6 0.0 copy-start.4
  0.6 0.0 copy-start.1
  0.6 0.8 copy.9.col_ref
  1.4 0.0 copy-done.4
  1.4 0.0 copy-done.1
  1.4 0.6 columns.1
  2.0 0.0 copy-start.2
  2.1 0.0 copy-start.3
  2.1 0.0 copy-start.5
  2.1 17.5 %all_to_all.30.got_ref = f32[32,8,128]{2,1,0:T(8,128)S(1)} all-to-all(f32[32,8,128]{2,1,0:T(8,128)S(1)} %columns.1), channel_id=1, replica_groups=mesh['xh'=2,'xl'=2,'yh'=2,'zh'=4,'zl'=4,'yl'=2,'co'=2] {'xh','xl','yh','..., dimensions={0} | all-to-all | bytes 262144 | tf_op jit(solution)/shard_map/all_to_all | solution.py:262
  19.5 0.0 copy-done.2
  19.5 0.0 copy-done.3
  19.5 0.6 rows.1
  20.2 25.1 %all_to_all.31.got_ref = f32[16,8,128]{2,1,0:T(8,128)S(1)} all-to-all(f32[16,8,128]{2,1,0:T(8,128)S(1)} %get-tuple-element.8), channel_id=1, replica_groups=mesh['xh'=2,'xl'=2,'yh'=2,'zh'=4,'zl'=4,'yl'=2,'co'=2] {'zh','zl'}, dimensions={0} | all-to-all | bytes 131072 | tf_op jit(solution)/shard_map/all_to_all | solution.py:262
  45.3 0.1 spread.1
  45.4 10.4 %all_to_all.32.got_ref = f32[16,4,128]{2,1,0:T(4,128)S(1)} all-to-all(f32[16,4,128]{2,1,0:T(4,128)S(1)} %spread.1), channel_id=1, replica_groups=mesh['xh'=2,'xl'=2,'yh'=2,'zh'=4,'zl'=4,'yl'=2,'co'=2] {'xl','yh','yl','..., dimensions={0} | all-to-all | bytes 65536 | tf_op jit(solution)/shard_map/all_to_all | solution.py:262
  55.7 0.0 copy-done.5
  55.7 0.1 copy.10.recon_ref
  55.8 0.7 slopes.1
  56.5 11.5 %all_to_all.33.got_ref = f32[32,2,256]{2,1,0:T(2,128)S(1)} all-to-all(f32[32,2,256]{2,1,0:T(2,128)S(1)} %get-tuple-element.12), channel_id=1, replica_groups=mesh['xh'=2,'xl'=2,'yh'=2,'zh'=4,'zl'=4,'yl'=2,'co'=2] {'xh','xl','yh','..., dimensions={0} | all-to-all | bytes 131072 | tf_op jit(solution)/shard_map/all_to_all | solution.py:262
  68.1 14.0 %all_to_all.34.got_ref = f32[16,2,256]{2,1,0:T(2,128)S(1)} all-to-all(f32[16,2,256]{2,1,0:T(2,128)S(1)} %sum_plane.1), channel_id=1, replica_groups=mesh['xh'=2,'xl'=2,'yh'=2,'zh'=4,'zl'=4,'yl'=2,'co'=2] {'zh','zl'}, dimensions={0} | all-to-all | bytes 65536 | tf_op jit(solution)/shard_map/all_to_all | solution.py:262
  82.1 0.0 copy-start
  82.2 12.3 %all_to_all.35.got_ref = f32[32,2,256]{2,1,0:T(2,128)S(1)} all-to-all(f32[32,2,256]{2,1,0:T(2,128)S(1)} %sum_ring.1), channel_id=1, replica_groups=mesh['xh'=2,'xl'=2,'yh'=2,'zh'=4,'zl'=4,'yl'=2,'co'=2] {'xh','xl','yh','..., dimensions={0} | all-to-all | bytes 131072 | tf_op jit(solution)/shard_map/all_to_all | solution.py:262
  94.4 0.0 copy-done
  94.4 0.7 clip.1
  (2 shorter events, 0.1 us)
Async XLA Ops:
  0.6 0.8 copy-start.4
  0.6 0.8 copy-start.1
  2.0 17.5 %copy-start.2 = (f32[16,25]{1,0:T(8,128)S(1)}, f32[16,25]{1,0:T(8,128)}, u32[]{:S(2)}) copy-start(f32[16,25]{1,0:T(8,128)} %light_ref.1) | copy-start | bytes 4804
  2.1 17.5 %copy-start.3 = (s32[2,16,2]{1,2,0:T(2,128)S(1)}, s32[2,16,2]{1,2,0:T(2,128)}, u32[]{:S(2)}) copy-start(s32[2,16,2]{1,2,0:T(2,128)} %param.8) | copy-start | bytes 772
  2.1 53.6 %copy-start.5 = (bf16[2,25,6000]{2,0,1:T(2,128)(2,1)S(1)}, bf16[2,25,6000]{2,0,1:T(2,128)(2,1)}, u32[]{:S(2)}) copy-start(bf16[2,25,6000]{2,0,1:T(2,128)(2,1)} %param.12) | copy-start | bytes 1800004
  82.1 12.3 %copy-start = (s32[6000]{0:T(1024)S(1)}, s32[6000]{0:T(1024)}, u32[]{:S(2)}) copy-start(s32[6000]{0:T(1024)} %code_ref.1) | copy-start | bytes 72004

commit v4 on v3

--- a/solution.py
+++ b/solution.py
@@ -220,12 +220,12 @@
         left = jnp.where(row == 0, compact[0][axis : axis + 1], compact[1][axis : axis + 1])
         left = left[:, 0:25].astype(BF16)
         total = total + jnp.dot(left, recon_ref[axis], preferred_element_type=F32)
-    for j in range(23):
-        out_ref[j] = total[0:2, 256 * j : 256 * j + 256]
-    out_ref[23] = jnp.zeros((2, 256), F32)
-    out_ref[23, :, 0:112] = total[0:2, 5888:6000]
-    for j in range(24, 32):
-        out_ref[j] = jnp.zeros((2, 256), F32)
+    for j in range(32):
+        start = 384 * (j % 16)
+        width = min(384, ACTUATORS - start)
+        if width < 384:
+            out_ref[j] = jnp.zeros((1, 384), F32)
+        out_ref[j, :, 0:width] = total[j // 16 : j // 16 + 1, start : start + width]
 
 
 def sum_kernel(got_ref, out_ref):
@@ -236,14 +236,14 @@
 
 def clip_kernel(got_ref, code_ref, slopes_ref, slopes_out, out_ref):
     slopes_out[...] = slopes_ref[:, 0:2, 0:25]
-    for j in range(24):
-        width = 256 if j < 23 else 112
-        update = got_ref[j][:, 0:width]
-        limit = code_ref[256 * j : 256 * j + width].reshape(1, width).astype(F32) * 0.125
-        first = jnp.clip(0.5 * update[0:1], -limit, limit)
-        second = jnp.clip(first + 0.5 * update[1:2], -limit, limit)
-        out_ref[0:1, 256 * j : 256 * j + width] = first
-        out_ref[1:2, 256 * j : 256 * j + width] = second
+    for j in range(16):
+        start = 384 * j
+        width = min(384, ACTUATORS - start)
+        limit = code_ref[start : start + width].reshape(1, width).astype(F32) * 0.125
+        first = jnp.clip(0.5 * got_ref[j][:, 0:width], -limit, limit)
+        second = jnp.clip(first + 0.5 * got_ref[16 + j][:, 0:width], -limit, limit)
+        out_ref[0:1, start : start + width] = first
+        out_ref[1:2, start : start + width] = second
 
 
 def call(body, outs, specs, *args, scratch=(), name=None):
@@ -284,7 +284,7 @@
     owned, reconstructor = lax.optimization_barrier((owned, reconstructor))
     slopes, updates = call(
         slopes_kernel,
-        (shape((2, 8, 128), F32), shape((32, 2, 256), F32)),
+        (shape((2, 8, 128), F32), shape((32, 1, 384), F32)),
         [VMEM, VMEM, VMEM],
         owned,
         light,
@@ -292,9 +292,9 @@
         name="slopes",
     )
     updates = exchange(updates, PLANE)
-    updates = call(sum_kernel, shape((16, 2, 256), F32), [VMEM], updates, name="sum_plane")
+    updates = call(sum_kernel, shape((16, 1, 384), F32), [VMEM], updates, name="sum_plane")
     updates = exchange(updates, RING)
-    updates = call(sum_kernel, shape((32, 2, 256), F32), [VMEM], updates, name="sum_ring")
+    updates = call(sum_kernel, shape((32, 1, 384), F32), [VMEM], updates, name="sum_ring")
     updates = exchange(updates, PLANE)
     return call(
         clip_kernel,

time: 95.5 us -> 95.3 us (level)
  no operation moved by 1% of the time
where the time goes in v4:
time: 95.3 us; the launch traced here: 94.9 us
  blocking collectives  90.6 us (95%)
  Pallas kernels  2.77 us (3%)
    all_to_all x6, blocking collectives, exchange(): return lax.all_to_all(value, axes, 0, 0, tiled=True)  90.6 us
    pallas_call x7, Pallas kernels, call(): pl.pallas_call(body, out_shape=outs, in_specs=specs, out_specs=jax.tree.m...  2.77 us

profile of v4, /device:TPU:1, one launch (start us, length us, event | category | flops | bytes accessed | tf_op | source)
XLA Modules:
  0.0 94.9 jit_solution(5634945907146724574)
XLA Ops:
  0.6 0.0 copy-start.4
  0.6 0.0 copy-start.1
  0.6 0.8 copy.9.col_ref
  1.4 0.0 copy-done.4
  1.4 0.0 copy-done.1
  1.4 0.6 columns.1
  2.0 0.0 copy-start.2
  2.1 0.0 copy-start.3
  2.1 0.0 copy-start.5
  2.1 17.5 %all_to_all.30.got_ref = f32[32,8,128]{2,1,0:T(8,128)S(1)} all-to-all(f32[32,8,128]{2,1,0:T(8,128)S(1)} %columns.1), channel_id=1, replica_groups=mesh['xh'=2,'xl'=2,'yh'=2,'zh'=4,'zl'=4,'yl'=2,'co'=2] {'xh','xl','yh','..., dimensions={0} | all-to-all | bytes 262144 | tf_op jit(solution)/shard_map/all_to_all | solution.py:262
  19.5 0.0 copy-done.2
  19.5 0.0 copy-done.3
  19.5 0.6 rows.1
  20.2 25.1 %all_to_all.31.got_ref = f32[16,8,128]{2,1,0:T(8,128)S(1)} all-to-all(f32[16,8,128]{2,1,0:T(8,128)S(1)} %get-tuple-element.8), channel_id=1, replica_groups=mesh['xh'=2,'xl'=2,'yh'=2,'zh'=4,'zl'=4,'yl'=2,'co'=2] {'zh','zl'}, dimensions={0} | all-to-all | bytes 131072 | tf_op jit(solution)/shard_map/all_to_all | solution.py:262
  45.3 0.1 spread.1
  45.4 10.4 %all_to_all.32.got_ref = f32[16,4,128]{2,1,0:T(4,128)S(1)} all-to-all(f32[16,4,128]{2,1,0:T(4,128)S(1)} %spread.1), channel_id=1, replica_groups=mesh['xh'=2,'xl'=2,'yh'=2,'zh'=4,'zl'=4,'yl'=2,'co'=2] {'xl','yh','yl','..., dimensions={0} | all-to-all | bytes 65536 | tf_op jit(solution)/shard_map/all_to_all | solution.py:262
  55.7 0.0 copy-done.5
  55.7 0.1 copy.10.recon_ref
  55.8 0.7 slopes.1
  56.5 11.5 %all_to_all.33.got_ref = f32[32,1,384]{2,1,0:T(1,128)S(1)} all-to-all(f32[32,1,384]{2,1,0:T(1,128)S(1)} %get-tuple-element.12), channel_id=1, replica_groups=mesh['xh'=2,'xl'=2,'yh'=2,'zh'=4,'zl'=4,'yl'=2,'co'=2] {'xh','xl','yh','..., dimensions={0} | all-to-all | bytes 98304 | tf_op jit(solution)/shard_map/all_to_all | solution.py:262
  68.1 14.0 %all_to_all.34.got_ref = f32[16,1,384]{2,1,0:T(1,128)S(1)} all-to-all(f32[16,1,384]{2,1,0:T(1,128)S(1)} %sum_plane.1), channel_id=1, replica_groups=mesh['xh'=2,'xl'=2,'yh'=2,'zh'=4,'zl'=4,'yl'=2,'co'=2] {'zh','zl'}, dimensions={0} | all-to-all | bytes 49152 | tf_op jit(solution)/shard_map/all_to_all | solution.py:262
  82.1 0.0 copy-start
  82.1 12.2 %all_to_all.35.got_ref = f32[32,1,384]{2,1,0:T(1,128)S(1)} all-to-all(f32[32,1,384]{2,1,0:T(1,128)S(1)} %sum_ring.1), channel_id=1, replica_groups=mesh['xh'=2,'xl'=2,'yh'=2,'zh'=4,'zl'=4,'yl'=2,'co'=2] {'xh','xl','yh','..., dimensions={0} | all-to-all | bytes 98304 | tf_op jit(solution)/shard_map/all_to_all | solution.py:262
  94.3 0.0 copy-done
  94.3 0.7 clip.1
  (2 shorter events, 0.1 us)
Async XLA Ops:
  0.6 0.8 copy-start.4
  0.6 0.8 copy-start.1
  2.0 17.5 %copy-start.2 = (f32[16,25]{1,0:T(8,128)S(1)}, f32[16,25]{1,0:T(8,128)}, u32[]{:S(2)}) copy-start(f32[16,25]{1,0:T(8,128)} %light_ref.1) | copy-start | bytes 4804
  2.1 17.5 %copy-start.3 = (s32[2,16,2]{1,2,0:T(2,128)S(1)}, s32[2,16,2]{1,2,0:T(2,128)}, u32[]{:S(2)}) copy-start(s32[2,16,2]{1,2,0:T(2,128)} %param.8) | copy-start | bytes 772
  2.1 53.6 %copy-start.5 = (bf16[2,25,6000]{2,0,1:T(2,128)(2,1)S(1)}, bf16[2,25,6000]{2,0,1:T(2,128)(2,1)}, u32[]{:S(2)}) copy-start(bf16[2,25,6000]{2,0,1:T(2,128)(2,1)} %param.12) | copy-start | bytes 1800004
  82.1 12.2 %copy-start = (s32[6000]{0:T(1024)S(1)}, s32[6000]{0:T(1024)}, u32[]{:S(2)}) copy-start(s32[6000]{0:T(1024)} %code_ref.1) | copy-start | bytes 72004

commit v5 on v4

--- a/solution.py
+++ b/solution.py
@@ -15,7 +15,7 @@
 ALT = ("xh", "xl", "yh")
 STRIP = ("zh", "zl", "yl", "co")
 PLANE = ("xh", "xl", "yh", "yl", "co")
-HALF = ("xl", "yh", "yl", "co")
+EIGHT = ("xl", "yl", "co")
 RING = ("zh", "zl")
 
 ROOT = 2.0**0.5
@@ -37,15 +37,16 @@
 
 
 def block_index():
-    return (lax.axis_index("xl") * 2 + lax.axis_index("yh")) * 4 + ylc_index()
+    return lax.axis_index("xl") * 4 + ylc_index()
 
 
 def columns_kernel(col_ref, bin_ref, screen_ref, out_ref):
     alt = alt_index()
     lane = iota((1, 512), 1)
-    block = lane >> 5
-    part = (lane & 31) >> 2
-    lenslet = jnp.where(part < 4, 20 * part + block, 20 * (block >> 2) + 16 + (block & 3))
+    block = lane >> 6
+    part = (lane & 63) >> 2
+    more = 20 * (block >> 1) + 16 + 2 * (block & 1)
+    lenslet = jnp.where(part < 8, 20 * (part >> 1) + 2 * block, more) + (part & 1)
     column = (4 * lenslet + (lane & 3)).astype(F32)
     position = iota((384, 512), 0).astype(F32)
     results = []
@@ -63,37 +64,36 @@
                 parts.append(turned[:, :384])
         stacked = jnp.concatenate(parts, axis=0).astype(BF16)
         results.append(jnp.dot(stacked, weights, preferred_element_type=F32))
-    group = iota((8, 128), 1) >> 5
+    left_half = iota((8, 128), 1) < 64
     for star in range(2):
-        for tile in range(4):
-            slots = []
+        for block in range(8):
+            start = (block // 2) * 128
             for layer in range(2):
-                for frame in range(2):
-                    top = (frame * 2 + star) * 8
-                    slots.append(results[layer][top : top + 8, tile * 128 : tile * 128 + 128])
-            for inner in range(4):
-                merged = jnp.zeros((8, 128), F32)
-                for slot in range(4):
-                    shift = (32 * (slot - inner)) % 128
-                    moved = slots[slot] if shift == 0 else pltpu.roll(slots[slot], shift, axis=1)
-                    merged = jnp.where(group == slot, moved, merged)
-                out_ref[star * 16 + tile * 4 + inner] = merged
+                zero = results[layer][star * 8 : star * 8 + 8, start : start + 128]
+                one = results[layer][16 + star * 8 : 24 + star * 8, start : start + 128]
+                if block % 2 == 0:
+                    one = pltpu.roll(one, 64, axis=1)
+                else:
+                    zero = pltpu.roll(zero, 64, axis=1)
+                merged = jnp.where(left_half, zero, one)
+                for yh in range(2):
+                    to = star * 16 + (block // 4) * 8 + yh * 4 + block % 4
+                    out_ref[to, :, layer * 128 : layer * 128 + 128] = merged
 
 
 def rows_kernel(row_ref, bin_ref, light_ref, got_ref, out_ref, light_out, scratch):
     star = lax.axis_index("xh")
     block = block_index()
     ring = lax.axis_index("zh") * 4 + lax.axis_index("zl")
-    values = got_ref[...].reshape(256, 128)
-    high = values.astype(BF16).astype(F32)
-    low = values - high
-    wide = iota((256, 128), 1)
+    values = got_ref[...].reshape(256, 256)
+    high = values.astype(BF16)
+    low = (values - high.astype(F32)).astype(BF16)
     rights = [
-        jnp.where(wide < 64, high, pltpu.roll(low, 64, axis=1)).astype(BF16),
-        jnp.where(wide < 64, pltpu.roll(high, 64, axis=1), low).astype(BF16),
+        jnp.concatenate([high[:, at : at + 128], low[:, at : at + 128]], axis=1) for at in (0, 128)
     ]
-    line = iota((64, 1), 0)
-    base = (80 * ((line >> 2) & 3) + 20 * (line >> 4) + (line & 3)).astype(F32)
+    line = iota((32, 1), 0)
+    quarter = 2 * ((line >> 2) & 1) + lax.axis_index("yh")
+    base = (80 * quarter + 20 * (line >> 3) + (line & 3)).astype(F32)
     pupil_row = jnp.concatenate([base + 4.0 * rr for rr in range(5)], axis=0)
     screen_row = (ring * 32 + (iota((1, 256), 1) & 31)).astype(F32)
     tops = [jnp.where(star == 0, row_ref[frame, 0:1, :], row_ref[frame, 1:2, :]) for frame in range(2)]
@@ -113,29 +113,22 @@
             weights = jnp.maximum(0.0, 1.0 - jnp.abs(offset - scaled)).astype(BF16)
             term = jnp.dot(weights, rights[layer], preferred_element_type=F32)
             sums[frame] = term if layer == 0 else sums[frame] + term
-    lane = iota((8, 128), 1)
-    cell = lane & 31
-    odd = (lane & 32) != 0
-    kind = jnp.where(cell < 16, cell >> 2, block >> 2)
+    sums = [total[:, :128] + total[:, 128:] for total in sums]
+    merged = jnp.where(iota((160, 128), 1) < 64, sums[0], sums[1])
+    cell = iota((8, 128), 1) & 63
+    kind = jnp.where(cell < 32, cell >> 3, block >> 1)
     for t in range(4):
-        pieces = []
-        for rr in range(5):
-            halves = []
-            for h in range(2):
-                start = rr * 64 + t * 16 + h * 8
-                both = jnp.where(odd, sums[1][start : start + 8], sums[0][start : start + 8])
-                halves.append(both + pltpu.roll(both, 64, axis=1))
-            pieces.append(jnp.where(lane < 64, halves[0], halves[1]))
+        pieces = [merged[rr * 32 + t * 8 : rr * 32 + t * 8 + 8] for rr in range(5)]
         for zl in range(4):
             here, after = pieces[zl], pieces[zl + 1]
             first = jnp.where(kind < zl, after, here)
-            second = jnp.where(cell < 24, pltpu.roll(after, 20 - 4 * zl, axis=1), pltpu.roll(after, 8, axis=1))
-            out_ref[t * 4 + zl] = jnp.where(cell < 20, first, second)
+            second = jnp.where(cell < 48, pltpu.roll(after, 40 - 8 * zl, axis=1), pltpu.roll(after, 16, axis=1))
+            out_ref[t * 4 + zl] = jnp.where(cell < 40, first, second)
     scratch[...] = jnp.ones((16, 128), F32)
     scratch[:, 0:25] = light_ref[...]
     wide = scratch[...]
     inside = iota((16, 128), 1)
-    scratch[...] = jnp.where((inside >= 32) & (inside < 57), pltpu.roll(wide, 32, axis=1), wide)
+    scratch[...] = jnp.where((inside >= 64) & (inside < 89), pltpu.roll(wide, 64, axis=1), wide)
     for q in range(4):
         top = (q % 2) * 4
         light_out[q // 2, top : top + 4, :] = scratch[pl.ds(q, 4, stride=4), :]
@@ -143,18 +136,16 @@
 
 def spread_kernel(got_ref, out_ref):
     total = jnp.sum(got_ref[...], axis=0)
-    turned = [total, pltpu.roll(total, 64, axis=1)]
-    for quarter in range(4):
-        piece = turned[quarter // 2][(quarter % 2) * 4 : (quarter % 2) * 4 + 4]
-        for ylc in range(4):
-            out_ref[quarter * 4 + ylc] = piece
+    for to in range(8):
+        top = (to // 4) * 4
+        out_ref[to] = total[top : top + 4]
 
 
 def slopes_kernel(got_ref, light_ref, recon_ref, slopes_ref, out_ref):
     zl = lax.axis_index("zl")
     row = iota((8, 128), 0)
     lane = iota((8, 128), 1)
-    cell = lane & 31
+    cell = lane & 63
     phases = [jnp.zeros((8, 128), F32), jnp.zeros((8, 128), F32)]
     flat_start = 100 * zl + 25 * ylc_index()
     for n in range(25):
@@ -164,9 +155,10 @@
         kind = (lens_col * 205) >> 12
         index = lens_col - 20 * kind
         regular = index < 16
-        source = jnp.where(regular, index, 4 * kind + index - 16)
+        source = jnp.where(regular, index >> 1, 2 * kind + ((index - 16) >> 1))
         first = lens_row == zl + (kind < zl).astype(I32)
-        place = jnp.where(regular, jnp.where(first, 4 * kind, 20), jnp.where(first, 16, 24))
+        unit = jnp.where(regular, jnp.where(first, 2 * kind, 10), jnp.where(first, 8, 12))
+        place = 4 * (unit + (index & 1))
         block = got_ref[source]
         block = jnp.concatenate([block, block], axis=0)
         turned = [pltpu.roll(block, (n + 128 - q - place) & 127, axis=1) for q in range(4)]
@@ -212,7 +204,7 @@
     slope_p = jnp.sum(along_p, axis=0, keepdims=True) * scale
     slope_q = jnp.sum(along_q, axis=0, keepdims=True) * scale
     pair = jnp.where(row == 0, slope_p, slope_q)
-    compact = [pair, pltpu.roll(pair, 96, axis=1)]
+    compact = [pair, pltpu.roll(pair, 64, axis=1)]
     for frame in range(2):
         slopes_ref[frame] = compact[frame]
     total = jnp.zeros((8, ACTUATORS), F32)
@@ -265,7 +257,7 @@
 def shards(screens, row_offset, col_offset, layer_bin, illumination, reconstructor, sat_code):
     shape = jax.ShapeDtypeStruct
     row_offset = jnp.transpose(row_offset, (0, 2, 1))
-    cols = call(columns_kernel, shape((32, 8, 128), F32), [VMEM, VMEM, VMEM], col_offset, layer_bin, screens, name="columns")
+    cols = call(columns_kernel, shape((32, 8, 256), F32), [VMEM, VMEM, VMEM], col_offset, layer_bin, screens, name="columns")
     cols = exchange(cols, PLANE)
     pupil, light = call(
         rows_kernel,
@@ -279,8 +271,8 @@
         name="rows",
     )
     pupil = exchange(pupil, RING)
-    owned = call(spread_kernel, shape((16, 4, 128), F32), [VMEM], pupil, name="spread")
-    owned = exchange(owned, HALF)
+    owned = call(spread_kernel, shape((8, 4, 128), F32), [VMEM], pupil, name="spread")
+    owned = exchange(owned, EIGHT)
     owned, reconstructor = lax.optimization_barrier((owned, reconstructor))
     slopes, updates = call(
         slopes_kernel,

time: 95.3 us -> 95 us (level)
  no operation moved by 1% of the time
where the time goes in v5:
time: 95 us; the launch traced here: 94.6 us
  blocking collectives  90.5 us (95%)
  Pallas kernels  2.52 us (3%)
    all_to_all x6, blocking collectives, exchange(): return lax.all_to_all(value, axes, 0, 0, tiled=True)  90.5 us
    pallas_call x7, Pallas kernels, call(): pl.pallas_call(body, out_shape=outs, in_specs=specs, out_specs=jax.tree.m...  2.52 us

profile of v5, /device:TPU:1, one launch (start us, length us, event | category | flops | bytes accessed | tf_op | source)
XLA Modules:
  0.0 94.6 jit_solution(8433969310228340515)
XLA Ops:
  0.6 0.0 copy-start.4
  0.6 0.0 copy-start.1
  0.6 0.8 copy.9.col_ref
  1.4 0.0 copy-done.4
  1.4 0.0 copy-done.1
  1.4 0.0 copy-start.5
  1.4 0.6 columns.1
  2.0 0.0 copy-start.2
  2.1 0.0 copy-start.3
  2.1 18.6 %all_to_all.30.got_ref = f32[32,8,256]{2,1,0:T(8,128)S(1)} all-to-all(f32[32,8,256]{2,1,0:T(8,128)S(1)} %columns.1), channel_id=1, replica_groups=mesh['xh'=2,'xl'=2,'yh'=2,'zh'=4,'zl'=4,'yl'=2,'co'=2] {'xh','xl','yh','..., dimensions={0} | all-to-all | bytes 524288 | tf_op jit(solution)/shard_map/all_to_all | solution.py:254
  20.7 0.0 copy-done.2
  20.7 0.0 copy-done.3
  20.7 0.5 rows.1
  21.1 25.1 %all_to_all.31.got_ref = f32[16,8,128]{2,1,0:T(8,128)S(1)} all-to-all(f32[16,8,128]{2,1,0:T(8,128)S(1)} %get-tuple-element.8), channel_id=1, replica_groups=mesh['xh'=2,'xl'=2,'yh'=2,'zh'=4,'zl'=4,'yl'=2,'co'=2] {'zh','zl'}, dimensions={0} | all-to-all | bytes 131072 | tf_op jit(solution)/shard_map/all_to_all | solution.py:254
  46.2 8.3 %all_to_all.32.got_ref = f32[8,4,128]{2,1,0:T(4,128)S(1)} all-to-all(f32[8,4,128]{2,1,0:T(4,128)S(1)} %spread.1), channel_id=1, replica_groups=mesh['xh'=2,'xl'=2,'yh'=2,'zh'=4,'zl'=4,'yl'=2,'co'=2] {'xl','yl','co'}, dimensions={0} | all-to-all | bytes 32768 | tf_op jit(solution)/shard_map/all_to_all | solution.py:254
  54.6 0.0 copy-done.5
  54.6 0.1 copy.10.recon_ref
  54.7 0.7 slopes.1
  55.4 12.3 %all_to_all.33.got_ref = f32[32,1,384]{2,1,0:T(1,128)S(1)} all-to-all(f32[32,1,384]{2,1,0:T(1,128)S(1)} %get-tuple-element.12), channel_id=1, replica_groups=mesh['xh'=2,'xl'=2,'yh'=2,'zh'=4,'zl'=4,'yl'=2,'co'=2] {'xh','xl','yh','..., dimensions={0} | all-to-all | bytes 98304 | tf_op jit(solution)/shard_map/all_to_all | solution.py:254
  67.7 14.0 %all_to_all.34.got_ref = f32[16,1,384]{2,1,0:T(1,128)S(1)} all-to-all(f32[16,1,384]{2,1,0:T(1,128)S(1)} %sum_plane.1), channel_id=1, replica_groups=mesh['xh'=2,'xl'=2,'yh'=2,'zh'=4,'zl'=4,'yl'=2,'co'=2] {'zh','zl'}, dimensions={0} | all-to-all | bytes 49152 | tf_op jit(solution)/shard_map/all_to_all | solution.py:254
  81.7 0.0 copy-start
  81.7 12.2 %all_to_all.35.got_ref = f32[32,1,384]{2,1,0:T(1,128)S(1)} all-to-all(f32[32,1,384]{2,1,0:T(1,128)S(1)} %sum_ring.1), channel_id=1, replica_groups=mesh['xh'=2,'xl'=2,'yh'=2,'zh'=4,'zl'=4,'yl'=2,'co'=2] {'xh','xl','yh','..., dimensions={0} | all-to-all | bytes 98304 | tf_op jit(solution)/shard_map/all_to_all | solution.py:254
  94.0 0.0 copy-done
  94.0 0.7 clip.1
  (3 shorter events, 0.1 us)
Async XLA Ops:
  0.6 0.8 copy-start.4
  0.6 0.8 copy-start.1
  1.4 53.1 %copy-start.5 = (bf16[2,25,6000]{2,0,1:T(2,128)(2,1)S(1)}, bf16[2,25,6000]{2,0,1:T(2,128)(2,1)}, u32[]{:S(2)}) copy-start(bf16[2,25,6000]{2,0,1:T(2,128)(2,1)} %param.12) | copy-start | bytes 1800004
  2.0 18.6 %copy-start.2 = (f32[16,25]{1,0:T(8,128)S(1)}, f32[16,25]{1,0:T(8,128)}, u32[]{:S(2)}) copy-start(f32[16,25]{1,0:T(8,128)} %light_ref.1) | copy-start | bytes 4804
  2.1 18.6 %copy-start.3 = (s32[2,16,2]{1,2,0:T(2,128)S(1)}, s32[2,16,2]{1,2,0:T(2,128)}, u32[]{:S(2)}) copy-start(s32[2,16,2]{1,2,0:T(2,128)} %param.8) | copy-start | bytes 772
  81.7 12.3 %copy-start = (s32[6000]{0:T(1024)S(1)}, s32[6000]{0:T(1024)}, u32[]{:S(2)}) copy-start(s32[6000]{0:T(1024)} %code_ref.1) | copy-start | bytes 72004

commit v6 on v5

--- a/solution.py
+++ b/solution.py
@@ -64,38 +64,48 @@
                 parts.append(turned[:, :384])
         stacked = jnp.concatenate(parts, axis=0).astype(BF16)
         results.append(jnp.dot(stacked, weights, preferred_element_type=F32))
-    left_half = iota((8, 128), 1) < 64
+    lane = iota((8, 128), 1)
     for star in range(2):
         for block in range(8):
             start = (block // 2) * 128
-            for layer in range(2):
-                zero = results[layer][star * 8 : star * 8 + 8, start : start + 128]
-                one = results[layer][16 + star * 8 : 24 + star * 8, start : start + 128]
-                if block % 2 == 0:
-                    one = pltpu.roll(one, 64, axis=1)
-                else:
-                    zero = pltpu.roll(zero, 64, axis=1)
-                merged = jnp.where(left_half, zero, one)
-                for yh in range(2):
-                    to = star * 16 + (block // 4) * 8 + yh * 4 + block % 4
-                    out_ref[to, :, layer * 128 : layer * 128 + 128] = merged
+            back = (block % 2) * 64
+
+            def piece(layer, frame, to):
+                top = frame * 16 + star * 8
+                value = results[layer][top : top + 8, start : start + 128]
+                shift = (to - back) % 128
+                return value if shift == 0 else pltpu.roll(value, shift, axis=1)
+
+            main = jnp.where(lane < 40, piece(0, 0, 0), jnp.where(lane < 80, piece(0, 1, 40), piece(1, 0, 80)))
+            rest = jnp.where(lane[0:4] < 64, piece(1, 1, 0)[0:4], piece(1, 1, 64)[4:8])
+            for yh in range(2):
+                to = star * 16 + (block // 4) * 8 + yh * 4 + block % 4
+                out_ref[to, 0] = main[0:4]
+                out_ref[to, 1] = main[4:8]
+                out_ref[to, 2] = rest
 
 
 def rows_kernel(row_ref, bin_ref, light_ref, got_ref, out_ref, light_out, scratch):
     star = lax.axis_index("xh")
     block = block_index()
     ring = lax.axis_index("zh") * 4 + lax.axis_index("zl")
-    values = got_ref[...].reshape(256, 256)
-    high = values.astype(BF16)
-    low = (values - high.astype(F32)).astype(BF16)
-    rights = [
-        jnp.concatenate([high[:, at : at + 128], low[:, at : at + 128]], axis=1) for at in (0, 128)
-    ]
+    main = jnp.concatenate([got_ref[:, half].reshape(128, 128) for half in range(2)], axis=0)
+    rest = got_ref[:, 2].reshape(128, 128)
+    rest = jnp.concatenate([pltpu.roll(rest, 64, axis=1), rest], axis=0)
+    left_half = iota((256, 128), 1) < 64
+    rights = []
+    for value in (
+        jnp.where(left_half, main, pltpu.roll(main, 24, axis=1)),
+        jnp.where(left_half, pltpu.roll(main, 48, axis=1), rest),
+    ):
+        high = value.astype(BF16)
+        rights.append(jnp.concatenate([high, (value - high.astype(F32)).astype(BF16)], axis=1))
     line = iota((32, 1), 0)
     quarter = 2 * ((line >> 2) & 1) + lax.axis_index("yh")
     base = (80 * quarter + 20 * (line >> 3) + (line & 3)).astype(F32)
     pupil_row = jnp.concatenate([base + 4.0 * rr for rr in range(5)], axis=0)
-    screen_row = (ring * 32 + (iota((1, 256), 1) & 31)).astype(F32)
+    spot = iota((1, 256), 1)
+    screen_row = (ring * 32 + 8 * ((spot >> 2) & 3) + 4 * (spot >> 7) + (spot & 3)).astype(F32)
     tops = [jnp.where(star == 0, row_ref[frame, 0:1, :], row_ref[frame, 1:2, :]) for frame in range(2)]
     parts = [top >> 4 for top in tops] + [top & 15 for top in tops] + [bin_ref[...].reshape(1, 16)]
     line16 = iota((8, 16), 0)
@@ -105,7 +115,7 @@
     packed = packed.astype(BF16)
     sums = [None, None]
     for layer in range(2):
-        pick = (iota((16, 256), 0) == 2 * (iota((16, 256), 1) >> 5) + layer).astype(F32).astype(BF16)
+        pick = (iota((16, 256), 0) == 2 * ((iota((16, 256), 1) >> 4) & 7) + layer).astype(F32).astype(BF16)
         lanes = jnp.dot(packed, pick, preferred_element_type=F32)
         scaled = pupil_row * (1.0 - lanes[4:5] * 0.03125)
         for frame in range(2):
@@ -257,7 +267,7 @@
 def shards(screens, row_offset, col_offset, layer_bin, illumination, reconstructor, sat_code):
     shape = jax.ShapeDtypeStruct
     row_offset = jnp.transpose(row_offset, (0, 2, 1))
-    cols = call(columns_kernel, shape((32, 8, 256), F32), [VMEM, VMEM, VMEM], col_offset, layer_bin, screens, name="columns")
+    cols = call(columns_kernel, shape((32, 3, 4, 128), F32), [VMEM, VMEM, VMEM], col_offset, layer_bin, screens, name="columns")
     cols = exchange(cols, PLANE)
     pupil, light = call(
         rows_kernel,

time: 95 us -> 94.4 us (level)
  no operation moved by 1% of the time
where the time goes in v6:
time: 94.4 us; the launch traced here: 94 us
  blocking collectives  89.8 us (95%)
  Pallas kernels  2.54 us (3%)
    all_to_all x6, blocking collectives, exchange(): return lax.all_to_all(value, axes, 0, 0, tiled=True)  89.8 us
    pallas_call x7, Pallas kernels, call(): pl.pallas_call(body, out_shape=outs, in_specs=specs, out_specs=jax.tree.m...  2.54 us

profile of v6, /device:TPU:1, one launch (start us, length us, event | category | flops | bytes accessed | tf_op | source)
XLA Modules:
  0.0 94.0 jit_solution(8764354411560848811)
XLA Ops:
  0.6 0.0 copy-start.4
  0.6 0.0 copy-start.1
  0.7 0.0 copy-start.5
  0.7 0.8 copy.9.col_ref
  1.5 0.0 copy-done.4
  1.5 0.0 copy-done.1
  1.5 0.6 columns.1
  2.1 0.0 copy-start.2
  2.1 0.0 copy-start.3
  2.1 17.9 %all_to_all.30.got_ref = f32[32,3,4,128]{3,2,1,0:T(4,128)S(1)} all-to-all(f32[32,3,4,128]{3,2,1,0:T(4,128)S(1)} %columns.1), channel_id=1, replica_groups=mesh['xh'=2,'xl'=2,'yh'=2,'zh'=4,'zl'=4,'yl'=2,'co'=2] {'xh','xl','yh','..., dimensions={0} | all-to-all | bytes 393216 | tf_op jit(solution)/shard_map/all_to_all | solution.py:264
  20.1 0.0 copy-done.2
  20.1 0.0 copy-done.3
  20.1 0.5 rows.1
  20.5 25.1 %all_to_all.31.got_ref = f32[16,8,128]{2,1,0:T(8,128)S(1)} all-to-all(f32[16,8,128]{2,1,0:T(8,128)S(1)} %get-tuple-element.8), channel_id=1, replica_groups=mesh['xh'=2,'xl'=2,'yh'=2,'zh'=4,'zl'=4,'yl'=2,'co'=2] {'zh','zl'}, dimensions={0} | all-to-all | bytes 131072 | tf_op jit(solution)/shard_map/all_to_all | solution.py:264
  45.6 8.4 %all_to_all.32.got_ref = f32[8,4,128]{2,1,0:T(4,128)S(1)} all-to-all(f32[8,4,128]{2,1,0:T(4,128)S(1)} %spread.1), channel_id=1, replica_groups=mesh['xh'=2,'xl'=2,'yh'=2,'zh'=4,'zl'=4,'yl'=2,'co'=2] {'xl','yl','co'}, dimensions={0} | all-to-all | bytes 32768 | tf_op jit(solution)/shard_map/all_to_all | solution.py:264
  54.1 0.0 copy-done.5
  54.1 0.1 copy.10.recon_ref
  54.1 0.7 slopes.1
  54.9 12.2 %all_to_all.33.got_ref = f32[32,1,384]{2,1,0:T(1,128)S(1)} all-to-all(f32[32,1,384]{2,1,0:T(1,128)S(1)} %get-tuple-element.12), channel_id=1, replica_groups=mesh['xh'=2,'xl'=2,'yh'=2,'zh'=4,'zl'=4,'yl'=2,'co'=2] {'xh','xl','yh','..., dimensions={0} | all-to-all | bytes 98304 | tf_op jit(solution)/shard_map/all_to_all | solution.py:264
  67.1 14.0 %all_to_all.34.got_ref = f32[16,1,384]{2,1,0:T(1,128)S(1)} all-to-all(f32[16,1,384]{2,1,0:T(1,128)S(1)} %sum_plane.1), channel_id=1, replica_groups=mesh['xh'=2,'xl'=2,'yh'=2,'zh'=4,'zl'=4,'yl'=2,'co'=2] {'zh','zl'}, dimensions={0} | all-to-all | bytes 49152 | tf_op jit(solution)/shard_map/all_to_all | solution.py:264
  81.1 0.0 copy-start
  81.2 12.2 %all_to_all.35.got_ref = f32[32,1,384]{2,1,0:T(1,128)S(1)} all-to-all(f32[32,1,384]{2,1,0:T(1,128)S(1)} %sum_ring.1), channel_id=1, replica_groups=mesh['xh'=2,'xl'=2,'yh'=2,'zh'=4,'zl'=4,'yl'=2,'co'=2] {'xh','xl','yh','..., dimensions={0} | all-to-all | bytes 98304 | tf_op jit(solution)/shard_map/all_to_all | solution.py:264
  93.4 0.0 copy-done
  93.4 0.7 clip.1
  (3 shorter events, 0.1 us)
Async XLA Ops:
  0.6 0.9 copy-start.4
  0.6 0.9 copy-start.1
  0.7 53.4 %copy-start.5 = (bf16[2,25,6000]{2,0,1:T(2,128)(2,1)S(1)}, bf16[2,25,6000]{2,0,1:T(2,128)(2,1)}, u32[]{:S(2)}) copy-start(bf16[2,25,6000]{2,0,1:T(2,128)(2,1)} %param.12) | copy-start | bytes 1800004
  2.1 18.0 %copy-start.2 = (f32[16,25]{1,0:T(8,128)S(1)}, f32[16,25]{1,0:T(8,128)}, u32[]{:S(2)}) copy-start(f32[16,25]{1,0:T(8,128)} %light_ref.1) | copy-start | bytes 4804
  2.1 18.0 %copy-start.3 = (s32[2,16,2]{1,2,0:T(2,128)S(1)}, s32[2,16,2]{1,2,0:T(2,128)}, u32[]{:S(2)}) copy-start(s32[2,16,2]{1,2,0:T(2,128)} %param.8) | copy-start | bytes 772
  81.1 12.2 %copy-start = (s32[6000]{0:T(1024)S(1)}, s32[6000]{0:T(1024)}, u32[]{:S(2)}) copy-start(s32[6000]{0:T(1024)} %code_ref.1) | copy-start | bytes 72004

commit v7 on v6

--- a/solution.py
+++ b/solution.py
@@ -151,30 +151,37 @@
         out_ref[to] = total[top : top + 4]
 
 
-def slopes_kernel(got_ref, light_ref, recon_ref, slopes_ref, out_ref):
+def slopes_kernel(got_ref, light_ref, recon_ref, slopes_ref, out_ref, scratch):
     zl = lax.axis_index("zl")
     row = iota((8, 128), 0)
     lane = iota((8, 128), 1)
-    cell = lane & 63
-    phases = [jnp.zeros((8, 128), F32), jnp.zeros((8, 128), F32)]
+    for source in range(8):
+        block = got_ref[source]
+        for q in range(4):
+            scratch[source, 4 * q : 4 * q + 4] = block if q == 0 else pltpu.roll(block, 128 - q, axis=1)
+    cell16 = iota((16, 128), 1) & 63
+    phase = jnp.zeros((16, 128), F32)
     flat_start = 100 * zl + 25 * ylc_index()
-    for n in range(25):
-        flat = flat_start + n
+    for five in range(5):
+        flat = flat_start + 5 * five
         lens_row = (flat * 205) >> 14
         lens_col = flat - 80 * lens_row
         kind = (lens_col * 205) >> 12
-        index = lens_col - 20 * kind
-        regular = index < 16
-        source = jnp.where(regular, index >> 1, 2 * kind + ((index - 16) >> 1))
+        start = lens_col - 20 * kind
         first = lens_row == zl + (kind < zl).astype(I32)
-        unit = jnp.where(regular, jnp.where(first, 2 * kind, 10), jnp.where(first, 8, 12))
-        place = 4 * (unit + (index & 1))
-        block = got_ref[source]
-        block = jnp.concatenate([block, block], axis=0)
-        turned = [pltpu.roll(block, (n + 128 - q - place) & 127, axis=1) for q in range(4)]
-        for h in range(2):
-            pair = jnp.where(row < 4, turned[2 * h], turned[2 * h + 1])
-            phases[h] = jnp.where(cell == n, pair, phases[h])
+        regular_place = jnp.where(first, 8 * kind, 40)
+        more_place = jnp.where(first, 32, 48)
+        inner = start < 15
+        for j in range(5):
+            n = 5 * five + j
+            index = start + j
+            source = index >> 1
+            place = regular_place + 4 * (index & 1)
+            if j > 0:
+                source = jnp.where(inner, source, 2 * kind + (j - 1) // 2)
+                place = jnp.where(inner, place, more_place + 4 * ((j - 1) % 2))
+            phase = jnp.where(cell16 == n, pltpu.roll(scratch[source], (n + 128 - place) & 127, axis=1), phase)
+    phases = [phase[0:8], phase[8:16]]
     re, im = [], []
     for h in range(2):
         light = light_ref[h]
@@ -291,6 +298,7 @@
         owned,
         light,
         reconstructor,
+        scratch=[pltpu.VMEM((8, 16, 128), F32)],
         name="slopes",
     )
     updates = exchange(updates, PLANE)

time: 94.4 us -> 94.3 us (level)
  no operation moved by 1% of the time
where the time goes in v7:
time: 94.3 us; the launch traced here: 93.9 us
  blocking collectives  89.8 us (95%)
  Pallas kernels  2.41 us (3%)
    all_to_all x6, blocking collectives, exchange(): return lax.all_to_all(value, axes, 0, 0, tiled=True)  89.8 us
    pallas_call x7, Pallas kernels, call(): pl.pallas_call(body, out_shape=outs, in_specs=specs, out_specs=jax.tree.m...  2.41 us

profile of v7, /device:TPU:1, one launch (start us, length us, event | category | flops | bytes accessed | tf_op | source)
XLA Modules:
  0.0 93.9 jit_solution(3937833015350353751)
XLA Ops:
  0.6 0.0 copy-start.4
  0.6 0.0 copy-start.1
  0.7 0.0 copy-start.5
  0.7 0.8 copy.9.col_ref
  1.5 0.0 copy-done.4
  1.5 0.0 copy-done.1
  1.5 0.6 columns.1
  2.1 0.0 copy-start.2
  2.1 0.0 copy-start.3
  2.1 17.9 %all_to_all.30.got_ref = f32[32,3,4,128]{3,2,1,0:T(4,128)S(1)} all-to-all(f32[32,3,4,128]{3,2,1,0:T(4,128)S(1)} %columns.1), channel_id=1, replica_groups=mesh['xh'=2,'xl'=2,'yh'=2,'zh'=4,'zl'=4,'yl'=2,'co'=2] {'xh','xl','yh','..., dimensions={0} | all-to-all | bytes 393216 | tf_op jit(solution)/shard_map/all_to_all | solution.py:271
  20.1 0.0 copy-done.2
  20.1 0.0 copy-done.3
  20.1 0.5 rows.1
  20.5 25.1 %all_to_all.31.got_ref = f32[16,8,128]{2,1,0:T(8,128)S(1)} all-to-all(f32[16,8,128]{2,1,0:T(8,128)S(1)} %get-tuple-element.8), channel_id=1, replica_groups=mesh['xh'=2,'xl'=2,'yh'=2,'zh'=4,'zl'=4,'yl'=2,'co'=2] {'zh','zl'}, dimensions={0} | all-to-all | bytes 131072 | tf_op jit(solution)/shard_map/all_to_all | solution.py:271
  45.6 8.4 %all_to_all.32.got_ref = f32[8,4,128]{2,1,0:T(4,128)S(1)} all-to-all(f32[8,4,128]{2,1,0:T(4,128)S(1)} %spread.1), channel_id=1, replica_groups=mesh['xh'=2,'xl'=2,'yh'=2,'zh'=4,'zl'=4,'yl'=2,'co'=2] {'xl','yl','co'}, dimensions={0} | all-to-all | bytes 32768 | tf_op jit(solution)/shard_map/all_to_all | solution.py:271
  54.1 0.0 copy-done.5
  54.1 0.1 copy.10.recon_ref
  54.1 0.6 slopes.1
  54.8 12.2 %all_to_all.33.got_ref = f32[32,1,384]{2,1,0:T(1,128)S(1)} all-to-all(f32[32,1,384]{2,1,0:T(1,128)S(1)} %get-tuple-element.12), channel_id=1, replica_groups=mesh['xh'=2,'xl'=2,'yh'=2,'zh'=4,'zl'=4,'yl'=2,'co'=2] {'xh','xl','yh','..., dimensions={0} | all-to-all | bytes 98304 | tf_op jit(solution)/shard_map/all_to_all | solution.py:271
  67.0 14.0 %all_to_all.34.got_ref = f32[16,1,384]{2,1,0:T(1,128)S(1)} all-to-all(f32[16,1,384]{2,1,0:T(1,128)S(1)} %sum_plane.1), channel_id=1, replica_groups=mesh['xh'=2,'xl'=2,'yh'=2,'zh'=4,'zl'=4,'yl'=2,'co'=2] {'zh','zl'}, dimensions={0} | all-to-all | bytes 49152 | tf_op jit(solution)/shard_map/all_to_all | solution.py:271
  81.0 0.0 copy-start
  81.0 12.2 %all_to_all.35.got_ref = f32[32,1,384]{2,1,0:T(1,128)S(1)} all-to-all(f32[32,1,384]{2,1,0:T(1,128)S(1)} %sum_ring.1), channel_id=1, replica_groups=mesh['xh'=2,'xl'=2,'yh'=2,'zh'=4,'zl'=4,'yl'=2,'co'=2] {'xh','xl','yh','..., dimensions={0} | all-to-all | bytes 98304 | tf_op jit(solution)/shard_map/all_to_all | solution.py:271
  93.2 0.0 copy-done
  93.2 0.7 clip.1
  (3 shorter events, 0.1 us)
Async XLA Ops:
  0.6 0.9 copy-start.4
  0.6 0.9 copy-start.1
  0.7 53.4 %copy-start.5 = (bf16[2,25,6000]{2,0,1:T(2,128)(2,1)S(1)}, bf16[2,25,6000]{2,0,1:T(2,128)(2,1)}, u32[]{:S(2)}) copy-start(bf16[2,25,6000]{2,0,1:T(2,128)(2,1)} %param.12) | copy-start | bytes 1800004
  2.1 18.0 %copy-start.2 = (f32[16,25]{1,0:T(8,128)S(1)}, f32[16,25]{1,0:T(8,128)}, u32[]{:S(2)}) copy-start(f32[16,25]{1,0:T(8,128)} %light_ref.1) | copy-start | bytes 4804
  2.1 18.0 %copy-start.3 = (s32[2,16,2]{1,2,0:T(2,128)S(1)}, s32[2,16,2]{1,2,0:T(2,128)}, u32[]{:S(2)}) copy-start(s32[2,16,2]{1,2,0:T(2,128)} %param.8) | copy-start | bytes 772
  81.0 12.2 %copy-start = (s32[6000]{0:T(1024)S(1)}, s32[6000]{0:T(1024)}, u32[]{:S(2)}) copy-start(s32[6000]{0:T(1024)} %code_ref.1) | copy-start | bytes 72004

commit v8 on v7

--- a/solution.py
+++ b/solution.py
@@ -125,7 +125,8 @@
             sums[frame] = term if layer == 0 else sums[frame] + term
     sums = [total[:, :128] + total[:, 128:] for total in sums]
     merged = jnp.where(iota((160, 128), 1) < 64, sums[0], sums[1])
-    cell = iota((8, 128), 1) & 63
+    lane = iota((8, 128), 1)
+    cell = lane & 63
     kind = jnp.where(cell < 32, cell >> 3, block >> 1)
     for t in range(4):
         pieces = [merged[rr * 32 + t * 8 : rr * 32 + t * 8 + 8] for rr in range(5)]
@@ -133,7 +134,12 @@
             here, after = pieces[zl], pieces[zl + 1]
             first = jnp.where(kind < zl, after, here)
             second = jnp.where(cell < 48, pltpu.roll(after, 40 - 8 * zl, axis=1), pltpu.roll(after, 16, axis=1))
-            out_ref[t * 4 + zl] = jnp.where(cell < 40, first, second)
+            value = jnp.where(cell < 40, first, second)
+            value = jnp.where(lane < 56, value, pltpu.roll(value, 120, axis=1))
+            last = pltpu.roll(jnp.broadcast_to(value[7:8], (8, 128)), 16, axis=1, stride=16, stride_axis=0)
+            value = jnp.where(lane < 112, value, last)
+            for n in range(7):
+                out_ref[t * 4 + zl, n] = value[n : n + 1]
     scratch[...] = jnp.ones((16, 128), F32)
     scratch[:, 0:25] = light_ref[...]
     wide = scratch[...]
@@ -144,8 +150,19 @@
         light_out[q // 2, top : top + 4, :] = scratch[pl.ds(q, 4, stride=4), :]
 
 
-def spread_kernel(got_ref, out_ref):
+def spread_kernel(got_ref, out_ref, scratch):
     total = jnp.sum(got_ref[...], axis=0)
+    scratch[...] = jnp.zeros((16, 128), F32)
+    for n in range(7):
+        scratch[n : n + 1] = total[n]
+        scratch[14 - n : 15 - n] = total[n]
+    total = scratch[0:8]
+    row = iota((8, 128), 0)
+    lane = iota((8, 128), 1)
+    ends = pltpu.roll(scratch[8:16], 16, axis=1, stride=16, stride_axis=0)
+    last = jnp.sum(jnp.where((lane >> 4) == row, ends, 0.0), axis=0, keepdims=True)
+    total = jnp.where(row == 7, last, total)
+    total = jnp.where(lane < 64, total, pltpu.roll(total, 8, axis=1))
     for to in range(8):
         top = (to // 4) * 4
         out_ref[to] = total[top : top + 4]
@@ -278,7 +295,7 @@
     cols = exchange(cols, PLANE)
     pupil, light = call(
         rows_kernel,
-        (shape((16, 8, 128), F32), shape((2, 8, 128), F32)),
+        (shape((16, 7, 1, 128), F32), shape((2, 8, 128), F32)),
         [VMEM, VMEM, VMEM, VMEM],
         row_offset,
         layer_bin,
@@ -288,7 +305,7 @@
         name="rows",
     )
     pupil = exchange(pupil, RING)
-    owned = call(spread_kernel, shape((8, 4, 128), F32), [VMEM], pupil, name="spread")
+    owned = call(spread_kernel, shape((8, 4, 128), F32), [VMEM], pupil, scratch=[pltpu.VMEM((16, 128), F32)], name="spread")
     owned = exchange(owned, EIGHT)
     owned, reconstructor = lax.optimization_barrier((owned, reconstructor))
     slopes, updates = call(

time: 94.3 us -> 94.2 us (level)
  no operation moved by 1% of the time
where the time goes in v8:
time: 94.2 us; the launch traced here: 93.8 us
  blocking collectives  89.5 us (95%)
  Pallas kernels  2.72 us (3%)
    all_to_all x6, blocking collectives, exchange(): return lax.all_to_all(value, axes, 0, 0, tiled=True)  89.5 us
    pallas_call x7, Pallas kernels, call(): pl.pallas_call(body, out_shape=outs, in_specs=specs, out_specs=jax.tree.m...  2.72 us

profile of v8, /device:TPU:1, one launch (start us, length us, event | category | flops | bytes accessed | tf_op | source)
XLA Modules:
  0.0 93.8 jit_solution(17627357534423114700)
XLA Ops:
  0.6 0.0 copy-start.4
  0.6 0.0 copy-start.1
  0.7 0.0 copy-start.5
  0.7 0.8 copy.9.col_ref
  1.5 0.0 copy-done.4
  1.5 0.0 copy-done.1
  1.5 0.6 columns.1
  2.1 0.0 copy-start.2
  2.1 0.0 copy-start.3
  2.1 17.9 %all_to_all.30.got_ref = f32[32,3,4,128]{3,2,1,0:T(4,128)S(1)} all-to-all(f32[32,3,4,128]{3,2,1,0:T(4,128)S(1)} %columns.1), channel_id=1, replica_groups=mesh['xh'=2,'xl'=2,'yh'=2,'zh'=4,'zl'=4,'yl'=2,'co'=2] {'xh','xl','yh','..., dimensions={0} | all-to-all | bytes 393216 | tf_op jit(solution)/shard_map/all_to_all | solution.py:288
  20.1 0.0 copy-done.2
  20.1 0.0 copy-done.3
  20.1 0.6 rows.1
  20.7 25.1 %all_to_all.31.got_ref = f32[16,7,1,128]{3,2,1,0:T(1,128)S(1)} all-to-all(f32[16,7,1,128]{3,2,1,0:T(1,128)S(1)} %get-tuple-element.8), channel_id=1, replica_groups=mesh['xh'=2,'xl'=2,'yh'=2,'zh'=4,'zl'=4,'yl'=2,'co'=2] {'zh','zl'}, dimensions={0} | all-to-all | bytes 114688 | tf_op jit(solution)/shard_map/all_to_all | solution.py:288
  45.8 0.2 spread.1
  46.0 8.3 %all_to_all.32.got_ref = f32[8,4,128]{2,1,0:T(4,128)S(1)} all-to-all(f32[8,4,128]{2,1,0:T(4,128)S(1)} %spread.1), channel_id=1, replica_groups=mesh['xh'=2,'xl'=2,'yh'=2,'zh'=4,'zl'=4,'yl'=2,'co'=2] {'xl','yl','co'}, dimensions={0} | all-to-all | bytes 32768 | tf_op jit(solution)/shard_map/all_to_all | solution.py:288
  54.3 0.0 copy-done.5
  54.3 0.1 copy.10.recon_ref
  54.4 0.6 slopes.1
  55.0 12.2 %all_to_all.33.got_ref = f32[32,1,384]{2,1,0:T(1,128)S(1)} all-to-all(f32[32,1,384]{2,1,0:T(1,128)S(1)} %get-tuple-element.12), channel_id=1, replica_groups=mesh['xh'=2,'xl'=2,'yh'=2,'zh'=4,'zl'=4,'yl'=2,'co'=2] {'xh','xl','yh','..., dimensions={0} | all-to-all | bytes 98304 | tf_op jit(solution)/shard_map/all_to_all | solution.py:288
  67.2 13.9 %all_to_all.34.got_ref = f32[16,1,384]{2,1,0:T(1,128)S(1)} all-to-all(f32[16,1,384]{2,1,0:T(1,128)S(1)} %sum_plane.1), channel_id=1, replica_groups=mesh['xh'=2,'xl'=2,'yh'=2,'zh'=4,'zl'=4,'yl'=2,'co'=2] {'zh','zl'}, dimensions={0} | all-to-all | bytes 49152 | tf_op jit(solution)/shard_map/all_to_all | solution.py:288
  81.2 0.0 copy-start
  81.2 12.0 %all_to_all.35.got_ref = f32[32,1,384]{2,1,0:T(1,128)S(1)} all-to-all(f32[32,1,384]{2,1,0:T(1,128)S(1)} %sum_ring.1), channel_id=1, replica_groups=mesh['xh'=2,'xl'=2,'yh'=2,'zh'=4,'zl'=4,'yl'=2,'co'=2] {'xh','xl','yh','..., dimensions={0} | all-to-all | bytes 98304 | tf_op jit(solution)/shard_map/all_to_all | solution.py:288
  93.2 0.0 copy-done
  93.2 0.7 clip.1
  (2 shorter events, 0.1 us)
Async XLA Ops:
  0.6 0.9 copy-start.4
  0.6 0.9 copy-start.1
  0.7 53.6 %copy-start.5 = (bf16[2,25,6000]{2,0,1:T(2,128)(2,1)S(1)}, bf16[2,25,6000]{2,0,1:T(2,128)(2,1)}, u32[]{:S(2)}) copy-start(bf16[2,25,6000]{2,0,1:T(2,128)(2,1)} %param.12) | copy-start | bytes 1800004
  2.1 18.0 %copy-start.2 = (f32[16,25]{1,0:T(8,128)S(1)}, f32[16,25]{1,0:T(8,128)}, u32[]{:S(2)}) copy-start(f32[16,25]{1,0:T(8,128)} %light_ref.1) | copy-start | bytes 4804
  2.1 18.0 %copy-start.3 = (s32[2,16,2]{1,2,0:T(2,128)S(1)}, s32[2,16,2]{1,2,0:T(2,128)}, u32[]{:S(2)}) copy-start(s32[2,16,2]{1,2,0:T(2,128)} %param.8) | copy-start | bytes 772
  81.2 12.0 %copy-start = (s32[6000]{0:T(1024)S(1)}, s32[6000]{0:T(1024)}, u32[]{:S(2)}) copy-start(s32[6000]{0:T(1024)} %code_ref.1) | copy-start | bytes 72004

commit v9 on v8

--- a/solution.py
+++ b/solution.py
@@ -26,6 +26,10 @@
 
 def iota(shape, dim):
     return lax.broadcasted_iota(I32, shape, dim)
+
+
+def tent(offset):
+    return jnp.maximum(BF16(0.0), BF16(1.0) - jnp.abs(offset.astype(BF16)))
 
 
 def alt_index():
@@ -55,7 +59,7 @@
     for layer in range(2):
         chosen = jnp.where(iota((1, 16), 1) == 2 * alt + layer, bins, 0).astype(F32)
         shrink = 1.0 - jnp.sum(chosen, axis=1, keepdims=True) * 0.03125
-        weights = jnp.maximum(0.0, 1.0 - jnp.abs(position - column * shrink)).astype(BF16)
+        weights = tent(position - column * shrink)
         rows = screen_ref[layer].astype(F32)
         parts = []
         for frame in range(2):
@@ -120,7 +124,7 @@
         scaled = pupil_row * (1.0 - lanes[4:5] * 0.03125)
         for frame in range(2):
             offset = screen_row - (16.0 * lanes[frame : frame + 1] + lanes[2 + frame : 3 + frame])
-            weights = jnp.maximum(0.0, 1.0 - jnp.abs(offset - scaled)).astype(BF16)
+            weights = tent(offset - scaled)
             term = jnp.dot(weights, rights[layer], preferred_element_type=F32)
             sums[frame] = term if layer == 0 else sums[frame] + term
     sums = [total[:, :128] + total[:, 128:] for total in sums]

time: 94.2 us -> 94.2 us (level)
  no operation moved by 1% of the time
where the time goes in v9:
time: 94.2 us; the launch traced here: 93.8 us
  blocking collectives  89.5 us (95%)
  Pallas kernels  2.67 us (3%)
    all_to_all x6, blocking collectives, exchange(): return lax.all_to_all(value, axes, 0, 0, tiled=True)  89.5 us
    pallas_call x7, Pallas kernels, call(): pl.pallas_call(body, out_shape=outs, in_specs=specs, out_specs=jax.tree.m...  2.67 us

profile of v9, /device:TPU:1, one launch (start us, length us, event | category | flops | bytes accessed | tf_op | source)
XLA Modules:
  0.0 93.8 jit_solution(8018537499975281784)
XLA Ops:
  0.6 0.0 copy-start.4
  0.6 0.0 copy-start.1
  0.7 0.0 copy-start.5
  0.7 0.8 copy.9.col_ref
  1.5 0.0 copy-done.4
  1.5 0.0 copy-done.1
  1.5 0.5 columns.1
  2.1 0.0 copy-start.2
  2.1 0.0 copy-start.3
  2.1 17.9 %all_to_all.30.got_ref = f32[32,3,4,128]{3,2,1,0:T(4,128)S(1)} all-to-all(f32[32,3,4,128]{3,2,1,0:T(4,128)S(1)} %columns.1), channel_id=1, replica_groups=mesh['xh'=2,'xl'=2,'yh'=2,'zh'=4,'zl'=4,'yl'=2,'co'=2] {'xh','xl','yh','..., dimensions={0} | all-to-all | bytes 393216 | tf_op jit(solution)/shard_map/all_to_all | solution.py:292
  20.0 0.0 copy-done.2
  20.0 0.0 copy-done.3
  20.0 0.6 rows.1
  20.6 25.1 %all_to_all.31.got_ref = f32[16,7,1,128]{3,2,1,0:T(1,128)S(1)} all-to-all(f32[16,7,1,128]{3,2,1,0:T(1,128)S(1)} %get-tuple-element.8), channel_id=1, replica_groups=mesh['xh'=2,'xl'=2,'yh'=2,'zh'=4,'zl'=4,'yl'=2,'co'=2] {'zh','zl'}, dimensions={0} | all-to-all | bytes 114688 | tf_op jit(solution)/shard_map/all_to_all | solution.py:292
  45.8 0.2 spread.1
  46.0 8.3 %all_to_all.32.got_ref = f32[8,4,128]{2,1,0:T(4,128)S(1)} all-to-all(f32[8,4,128]{2,1,0:T(4,128)S(1)} %spread.1), channel_id=1, replica_groups=mesh['xh'=2,'xl'=2,'yh'=2,'zh'=4,'zl'=4,'yl'=2,'co'=2] {'xl','yl','co'}, dimensions={0} | all-to-all | bytes 32768 | tf_op jit(solution)/shard_map/all_to_all | solution.py:292
  54.2 0.0 copy-done.5
  54.2 0.1 copy.10.recon_ref
  54.3 0.6 slopes.1
  54.9 12.2 %all_to_all.33.got_ref = f32[32,1,384]{2,1,0:T(1,128)S(1)} all-to-all(f32[32,1,384]{2,1,0:T(1,128)S(1)} %get-tuple-element.12), channel_id=1, replica_groups=mesh['xh'=2,'xl'=2,'yh'=2,'zh'=4,'zl'=4,'yl'=2,'co'=2] {'xh','xl','yh','..., dimensions={0} | all-to-all | bytes 98304 | tf_op jit(solution)/shard_map/all_to_all | solution.py:292
  67.2 13.9 %all_to_all.34.got_ref = f32[16,1,384]{2,1,0:T(1,128)S(1)} all-to-all(f32[16,1,384]{2,1,0:T(1,128)S(1)} %sum_plane.1), channel_id=1, replica_groups=mesh['xh'=2,'xl'=2,'yh'=2,'zh'=4,'zl'=4,'yl'=2,'co'=2] {'zh','zl'}, dimensions={0} | all-to-all | bytes 49152 | tf_op jit(solution)/shard_map/all_to_all | solution.py:292
  81.1 0.0 copy-start
  81.1 12.0 %all_to_all.35.got_ref = f32[32,1,384]{2,1,0:T(1,128)S(1)} all-to-all(f32[32,1,384]{2,1,0:T(1,128)S(1)} %sum_ring.1), channel_id=1, replica_groups=mesh['xh'=2,'xl'=2,'yh'=2,'zh'=4,'zl'=4,'yl'=2,'co'=2] {'xh','xl','yh','..., dimensions={0} | all-to-all | bytes 98304 | tf_op jit(solution)/shard_map/all_to_all | solution.py:292
  93.1 0.0 copy-done
  93.1 0.7 clip.1
  (2 shorter events, 0.1 us)
Async XLA Ops:
  0.6 0.9 copy-start.4
  0.6 0.9 copy-start.1
  0.7 53.6 %copy-start.5 = (bf16[2,25,6000]{2,0,1:T(2,128)(2,1)S(1)}, bf16[2,25,6000]{2,0,1:T(2,128)(2,1)}, u32[]{:S(2)}) copy-start(bf16[2,25,6000]{2,0,1:T(2,128)(2,1)} %param.12) | copy-start | bytes 1800004
  2.1 18.0 %copy-start.2 = (f32[16,25]{1,0:T(8,128)S(1)}, f32[16,25]{1,0:T(8,128)}, u32[]{:S(2)}) copy-start(f32[16,25]{1,0:T(8,128)} %light_ref.1) | copy-start | bytes 4804
  2.1 18.0 %copy-start.3 = (s32[2,16,2]{1,2,0:T(2,128)S(1)}, s32[2,16,2]{1,2,0:T(2,128)}, u32[]{:S(2)}) copy-start(s32[2,16,2]{1,2,0:T(2,128)} %param.8) | copy-start | bytes 772
  81.1 12.0 %copy-start = (s32[6000]{0:T(1024)S(1)}, s32[6000]{0:T(1024)}, u32[]{:S(2)}) copy-start(s32[6000]{0:T(1024)} %code_ref.1) | copy-start | bytes 72004

commit v10 on v9

--- a/solution.py
+++ b/solution.py
@@ -95,11 +95,11 @@
     ring = lax.axis_index("zh") * 4 + lax.axis_index("zl")
     main = jnp.concatenate([got_ref[:, half].reshape(128, 128) for half in range(2)], axis=0)
     rest = got_ref[:, 2].reshape(128, 128)
-    rest = jnp.concatenate([pltpu.roll(rest, 64, axis=1), rest], axis=0)
-    left_half = iota((256, 128), 1) < 64
+    rest = jnp.concatenate([pltpu.roll(rest, 56, axis=1), pltpu.roll(rest, 120, axis=1)], axis=0)
+    left_half = iota((256, 128), 1) < 56
     rights = []
     for value in (
-        jnp.where(left_half, main, pltpu.roll(main, 24, axis=1)),
+        jnp.where(left_half, main, pltpu.roll(main, 16, axis=1)),
         jnp.where(left_half, pltpu.roll(main, 48, axis=1), rest),
     ):
         high = value.astype(BF16)
@@ -128,9 +128,9 @@
             term = jnp.dot(weights, rights[layer], preferred_element_type=F32)
             sums[frame] = term if layer == 0 else sums[frame] + term
     sums = [total[:, :128] + total[:, 128:] for total in sums]
-    merged = jnp.where(iota((160, 128), 1) < 64, sums[0], sums[1])
+    merged = jnp.where(iota((160, 128), 1) < 56, sums[0], sums[1])
     lane = iota((8, 128), 1)
-    cell = lane & 63
+    cell = jnp.where(lane < 56, lane, lane - 56)
     kind = jnp.where(cell < 32, cell >> 3, block >> 1)
     for t in range(4):
         pieces = [merged[rr * 32 + t * 8 : rr * 32 + t * 8 + 8] for rr in range(5)]
@@ -139,7 +139,6 @@
             first = jnp.where(kind < zl, after, here)
             second = jnp.where(cell < 48, pltpu.roll(after, 40 - 8 * zl, axis=1), pltpu.roll(after, 16, axis=1))
             value = jnp.where(cell < 40, first, second)
-            value = jnp.where(lane < 56, value, pltpu.roll(value, 120, axis=1))
             last = pltpu.roll(jnp.broadcast_to(value[7:8], (8, 128)), 16, axis=1, stride=16, stride_axis=0)
             value = jnp.where(lane < 112, value, last)
             for n in range(7):

time: 94.2 us -> 94.1 us (level)
  no operation moved by 1% of the time
where the time goes in v10:
time: 94.1 us; the launch traced here: 93.7 us
  blocking collectives  89.5 us (95%)
  Pallas kernels  2.59 us (3%)
    all_to_all x6, blocking collectives, exchange(): return lax.all_to_all(value, axes, 0, 0, tiled=True)  89.5 us
    pallas_call x7, Pallas kernels, call(): pl.pallas_call(body, out_shape=outs, in_specs=specs, out_specs=jax.tree.m...  2.59 us

profile of v10, /device:TPU:1, one launch (start us, length us, event | category | flops | bytes accessed | tf_op | source)
XLA Modules:
  0.0 93.7 jit_solution(12168424855482467100)
XLA Ops:
  0.6 0.0 copy-start.4
  0.6 0.0 copy-start.1
  0.7 0.0 copy-start.5
  0.7 0.8 copy.9.col_ref
  1.5 0.0 copy-done.4
  1.5 0.0 copy-done.1
  1.5 0.5 columns.1
  2.1 0.0 copy-start.2
  2.1 0.0 copy-start.3
  2.1 17.9 %all_to_all.30.got_ref = f32[32,3,4,128]{3,2,1,0:T(4,128)S(1)} all-to-all(f32[32,3,4,128]{3,2,1,0:T(4,128)S(1)} %columns.1), channel_id=1, replica_groups=mesh['xh'=2,'xl'=2,'yh'=2,'zh'=4,'zl'=4,'yl'=2,'co'=2] {'xh','xl','yh','..., dimensions={0} | all-to-all | bytes 393216 | tf_op jit(solution)/shard_map/all_to_all | solution.py:291
  20.0 0.0 copy-done.2
  20.0 0.0 copy-done.3
  20.0 0.5 rows.1
  20.6 25.1 %all_to_all.31.got_ref = f32[16,7,1,128]{3,2,1,0:T(1,128)S(1)} all-to-all(f32[16,7,1,128]{3,2,1,0:T(1,128)S(1)} %get-tuple-element.8), channel_id=1, replica_groups=mesh['xh'=2,'xl'=2,'yh'=2,'zh'=4,'zl'=4,'yl'=2,'co'=2] {'zh','zl'}, dimensions={0} | all-to-all | bytes 114688 | tf_op jit(solution)/shard_map/all_to_all | solution.py:291
  45.7 0.2 spread.1
  45.9 8.3 %all_to_all.32.got_ref = f32[8,4,128]{2,1,0:T(4,128)S(1)} all-to-all(f32[8,4,128]{2,1,0:T(4,128)S(1)} %spread.1), channel_id=1, replica_groups=mesh['xh'=2,'xl'=2,'yh'=2,'zh'=4,'zl'=4,'yl'=2,'co'=2] {'xl','yl','co'}, dimensions={0} | all-to-all | bytes 32768 | tf_op jit(solution)/shard_map/all_to_all | solution.py:291
  54.2 0.0 copy-done.5
  54.2 0.1 copy.10.recon_ref
  54.2 0.6 slopes.1
  54.9 12.2 %all_to_all.33.got_ref = f32[32,1,384]{2,1,0:T(1,128)S(1)} all-to-all(f32[32,1,384]{2,1,0:T(1,128)S(1)} %get-tuple-element.12), channel_id=1, replica_groups=mesh['xh'=2,'xl'=2,'yh'=2,'zh'=4,'zl'=4,'yl'=2,'co'=2] {'xh','xl','yh','..., dimensions={0} | all-to-all | bytes 98304 | tf_op jit(solution)/shard_map/all_to_all | solution.py:291
  67.1 13.9 %all_to_all.34.got_ref = f32[16,1,384]{2,1,0:T(1,128)S(1)} all-to-all(f32[16,1,384]{2,1,0:T(1,128)S(1)} %sum_plane.1), channel_id=1, replica_groups=mesh['xh'=2,'xl'=2,'yh'=2,'zh'=4,'zl'=4,'yl'=2,'co'=2] {'zh','zl'}, dimensions={0} | all-to-all | bytes 49152 | tf_op jit(solution)/shard_map/all_to_all | solution.py:291
  81.1 0.0 copy-start
  81.1 12.0 %all_to_all.35.got_ref = f32[32,1,384]{2,1,0:T(1,128)S(1)} all-to-all(f32[32,1,384]{2,1,0:T(1,128)S(1)} %sum_ring.1), channel_id=1, replica_groups=mesh['xh'=2,'xl'=2,'yh'=2,'zh'=4,'zl'=4,'yl'=2,'co'=2] {'xh','xl','yh','..., dimensions={0} | all-to-all | bytes 98304 | tf_op jit(solution)/shard_map/all_to_all | solution.py:291
  93.1 0.0 copy-done
  93.1 0.7 clip.1
  (2 shorter events, 0.1 us)
Async XLA Ops:
  0.6 0.9 copy-start.4
  0.6 0.9 copy-start.1
  0.7 53.5 %copy-start.5 = (bf16[2,25,6000]{2,0,1:T(2,128)(2,1)S(1)}, bf16[2,25,6000]{2,0,1:T(2,128)(2,1)}, u32[]{:S(2)}) copy-start(bf16[2,25,6000]{2,0,1:T(2,128)(2,1)} %param.12) | copy-start | bytes 1800004
  2.1 18.0 %copy-start.2 = (f32[16,25]{1,0:T(8,128)S(1)}, f32[16,25]{1,0:T(8,128)}, u32[]{:S(2)}) copy-start(f32[16,25]{1,0:T(8,128)} %light_ref.1) | copy-start | bytes 4804
  2.1 18.0 %copy-start.3 = (s32[2,16,2]{1,2,0:T(2,128)S(1)}, s32[2,16,2]{1,2,0:T(2,128)}, u32[]{:S(2)}) copy-start(s32[2,16,2]{1,2,0:T(2,128)} %param.8) | copy-start | bytes 772
  81.1 12.0 %copy-start = (s32[6000]{0:T(1024)S(1)}, s32[6000]{0:T(1024)}, u32[]{:S(2)}) copy-start(s32[6000]{0:T(1024)} %code_ref.1) | copy-start | bytes 72004

commit v11 on v10

--- a/solution.py
+++ b/solution.py
@@ -52,7 +52,7 @@
     more = 20 * (block >> 1) + 16 + 2 * (block & 1)
     lenslet = jnp.where(part < 8, 20 * (part >> 1) + 2 * block, more) + (part & 1)
     column = (4 * lenslet + (lane & 3)).astype(F32)
-    position = iota((384, 512), 0).astype(F32)
+    position = iota((336, 512), 0).astype(F32)
     results = []
     bins = bin_ref[...].reshape(1, 16)
     lefts = [col_ref[frame, pl.ds(2 * alt, 2), :] for frame in range(2)]
@@ -65,7 +65,7 @@
         for frame in range(2):
             for star in range(2):
                 turned = pltpu.roll(rows, (512 - lefts[frame][layer, star]) & 511, axis=1)
-                parts.append(turned[:, :384])
+                parts.append(turned[:, :336])
         stacked = jnp.concatenate(parts, axis=0).astype(BF16)
         results.append(jnp.dot(stacked, weights, preferred_element_type=F32))
     lane = iota((8, 128), 1)

time: 94.1 us -> 94.1 us (level)
  no operation moved by 1% of the time
where the time goes in v11:
time: 94.1 us; the launch traced here: 93.7 us
  blocking collectives  89.5 us (95%)
  Pallas kernels  2.56 us (3%)
    all_to_all x6, blocking collectives, exchange(): return lax.all_to_all(value, axes, 0, 0, tiled=True)  89.5 us
    pallas_call x7, Pallas kernels, call(): pl.pallas_call(body, out_shape=outs, in_specs=specs, out_specs=jax.tree.m...  2.56 us

profile of v11, /device:TPU:1, one launch (start us, length us, event | category | flops | bytes accessed | tf_op | source)
XLA Modules:
  0.0 93.7 jit_solution(14147071077743338375)
XLA Ops:
  0.6 0.0 copy-start.4
  0.6 0.0 copy-start.1
  0.7 0.0 copy-start.5
  0.7 0.8 copy.9.col_ref
  1.5 0.0 copy-done.4
  1.5 0.0 copy-done.1
  1.5 0.5 columns.1
  2.0 0.0 copy-start.2
  2.0 0.0 copy-start.3
  2.0 17.9 %all_to_all.30.got_ref = f32[32,3,4,128]{3,2,1,0:T(4,128)S(1)} all-to-all(f32[32,3,4,128]{3,2,1,0:T(4,128)S(1)} %columns.1), channel_id=1, replica_groups=mesh['xh'=2,'xl'=2,'yh'=2,'zh'=4,'zl'=4,'yl'=2,'co'=2] {'xh','xl','yh','..., dimensions={0} | all-to-all | bytes 393216 | tf_op jit(solution)/shard_map/all_to_all | solution.py:291
  20.0 0.0 copy-done.2
  20.0 0.0 copy-done.3
  20.0 0.5 rows.1
  20.5 25.1 %all_to_all.31.got_ref = f32[16,7,1,128]{3,2,1,0:T(1,128)S(1)} all-to-all(f32[16,7,1,128]{3,2,1,0:T(1,128)S(1)} %get-tuple-element.8), channel_id=1, replica_groups=mesh['xh'=2,'xl'=2,'yh'=2,'zh'=4,'zl'=4,'yl'=2,'co'=2] {'zh','zl'}, dimensions={0} | all-to-all | bytes 114688 | tf_op jit(solution)/shard_map/all_to_all | solution.py:291
  45.7 0.2 spread.1
  45.9 8.3 %all_to_all.32.got_ref = f32[8,4,128]{2,1,0:T(4,128)S(1)} all-to-all(f32[8,4,128]{2,1,0:T(4,128)S(1)} %spread.1), channel_id=1, replica_groups=mesh['xh'=2,'xl'=2,'yh'=2,'zh'=4,'zl'=4,'yl'=2,'co'=2] {'xl','yl','co'}, dimensions={0} | all-to-all | bytes 32768 | tf_op jit(solution)/shard_map/all_to_all | solution.py:291
  54.1 0.0 copy-done.5
  54.1 0.1 copy.10.recon_ref
  54.2 0.6 slopes.1
  54.8 12.2 %all_to_all.33.got_ref = f32[32,1,384]{2,1,0:T(1,128)S(1)} all-to-all(f32[32,1,384]{2,1,0:T(1,128)S(1)} %get-tuple-element.12), channel_id=1, replica_groups=mesh['xh'=2,'xl'=2,'yh'=2,'zh'=4,'zl'=4,'yl'=2,'co'=2] {'xh','xl','yh','..., dimensions={0} | all-to-all | bytes 98304 | tf_op jit(solution)/shard_map/all_to_all | solution.py:291
  67.1 13.9 %all_to_all.34.got_ref = f32[16,1,384]{2,1,0:T(1,128)S(1)} all-to-all(f32[16,1,384]{2,1,0:T(1,128)S(1)} %sum_plane.1), channel_id=1, replica_groups=mesh['xh'=2,'xl'=2,'yh'=2,'zh'=4,'zl'=4,'yl'=2,'co'=2] {'zh','zl'}, dimensions={0} | all-to-all | bytes 49152 | tf_op jit(solution)/shard_map/all_to_all | solution.py:291
  81.0 0.0 copy-start
  81.0 12.0 %all_to_all.35.got_ref = f32[32,1,384]{2,1,0:T(1,128)S(1)} all-to-all(f32[32,1,384]{2,1,0:T(1,128)S(1)} %sum_ring.1), channel_id=1, replica_groups=mesh['xh'=2,'xl'=2,'yh'=2,'zh'=4,'zl'=4,'yl'=2,'co'=2] {'xh','xl','yh','..., dimensions={0} | all-to-all | bytes 98304 | tf_op jit(solution)/shard_map/all_to_all | solution.py:291
  93.0 0.0 copy-done
  93.0 0.7 clip.1
  (2 shorter events, 0.1 us)
Async XLA Ops:
  0.6 0.9 copy-start.4
  0.6 0.9 copy-start.1
  0.7 53.5 %copy-start.5 = (bf16[2,25,6000]{2,0,1:T(2,128)(2,1)S(1)}, bf16[2,25,6000]{2,0,1:T(2,128)(2,1)}, u32[]{:S(2)}) copy-start(bf16[2,25,6000]{2,0,1:T(2,128)(2,1)} %param.12) | copy-start | bytes 1800004
  2.0 18.0 %copy-start.2 = (f32[16,25]{1,0:T(8,128)S(1)}, f32[16,25]{1,0:T(8,128)}, u32[]{:S(2)}) copy-start(f32[16,25]{1,0:T(8,128)} %light_ref.1) | copy-start | bytes 4804
  2.0 18.0 %copy-start.3 = (s32[2,16,2]{1,2,0:T(2,128)S(1)}, s32[2,16,2]{1,2,0:T(2,128)}, u32[]{:S(2)}) copy-start(s32[2,16,2]{1,2,0:T(2,128)} %param.8) | copy-start | bytes 772
  81.0 12.0 %copy-start = (s32[6000]{0:T(1024)S(1)}, s32[6000]{0:T(1024)}, u32[]{:S(2)}) copy-start(s32[6000]{0:T(1024)} %code_ref.1) | copy-start | bytes 72004

commit v12 on v11

--- a/solution.py
+++ b/solution.py
@@ -52,7 +52,7 @@
     more = 20 * (block >> 1) + 16 + 2 * (block & 1)
     lenslet = jnp.where(part < 8, 20 * (part >> 1) + 2 * block, more) + (part & 1)
     column = (4 * lenslet + (lane & 3)).astype(F32)
-    position = iota((336, 512), 0).astype(F32)
+    position = iota((320, 512), 0).astype(F32)
     results = []
     bins = bin_ref[...].reshape(1, 16)
     lefts = [col_ref[frame, pl.ds(2 * alt, 2), :] for frame in range(2)]
@@ -65,7 +65,7 @@
         for frame in range(2):
             for star in range(2):
                 turned = pltpu.roll(rows, (512 - lefts[frame][layer, star]) & 511, axis=1)
-                parts.append(turned[:, :336])
+                parts.append(turned[:, :320])
         stacked = jnp.concatenate(parts, axis=0).astype(BF16)
         results.append(jnp.dot(stacked, weights, preferred_element_type=F32))
     lane = iota((8, 128), 1)

time: 94.1 us -> 94.1 us (level)
  no operation moved by 1% of the time
where the time goes in v12:
time: 94.1 us; the launch traced here: 93.7 us
  blocking collectives  89.5 us (95%)
  Pallas kernels  2.54 us (3%)
    all_to_all x6, blocking collectives, exchange(): return lax.all_to_all(value, axes, 0, 0, tiled=True)  89.5 us
    pallas_call x7, Pallas kernels, call(): pl.pallas_call(body, out_shape=outs, in_specs=specs, out_specs=jax.tree.m...  2.54 us

profile of v12, /device:TPU:1, one launch (start us, length us, event | category | flops | bytes accessed | tf_op | source)
XLA Modules:
  0.0 93.7 jit_solution(8938127202995916955)
XLA Ops:
  0.6 0.0 copy-start.4
  0.6 0.0 copy-start.1
  0.7 0.0 copy-start.5
  0.7 0.8 copy.9.col_ref
  1.5 0.0 copy-done.4
  1.5 0.0 copy-done.1
  1.5 0.5 columns.1
  2.0 0.0 copy-start.2
  2.0 0.0 copy-start.3
  2.0 17.9 %all_to_all.30.got_ref = f32[32,3,4,128]{3,2,1,0:T(4,128)S(1)} all-to-all(f32[32,3,4,128]{3,2,1,0:T(4,128)S(1)} %columns.1), channel_id=1, replica_groups=mesh['xh'=2,'xl'=2,'yh'=2,'zh'=4,'zl'=4,'yl'=2,'co'=2] {'xh','xl','yh','..., dimensions={0} | all-to-all | bytes 393216 | tf_op jit(solution)/shard_map/all_to_all | solution.py:291
  20.0 0.0 copy-done.2
  20.0 0.0 copy-done.3
  20.0 0.5 rows.1
  20.5 25.1 %all_to_all.31.got_ref = f32[16,7,1,128]{3,2,1,0:T(1,128)S(1)} all-to-all(f32[16,7,1,128]{3,2,1,0:T(1,128)S(1)} %get-tuple-element.8), channel_id=1, replica_groups=mesh['xh'=2,'xl'=2,'yh'=2,'zh'=4,'zl'=4,'yl'=2,'co'=2] {'zh','zl'}, dimensions={0} | all-to-all | bytes 114688 | tf_op jit(solution)/shard_map/all_to_all | solution.py:291
  45.6 0.2 spread.1
  45.8 8.3 %all_to_all.32.got_ref = f32[8,4,128]{2,1,0:T(4,128)S(1)} all-to-all(f32[8,4,128]{2,1,0:T(4,128)S(1)} %spread.1), channel_id=1, replica_groups=mesh['xh'=2,'xl'=2,'yh'=2,'zh'=4,'zl'=4,'yl'=2,'co'=2] {'xl','yl','co'}, dimensions={0} | all-to-all | bytes 32768 | tf_op jit(solution)/shard_map/all_to_all | solution.py:291
  54.1 0.0 copy-done.5
  54.1 0.1 copy.10.recon_ref
  54.2 0.6 slopes.1
  54.8 12.2 %all_to_all.33.got_ref = f32[32,1,384]{2,1,0:T(1,128)S(1)} all-to-all(f32[32,1,384]{2,1,0:T(1,128)S(1)} %get-tuple-element.12), channel_id=1, replica_groups=mesh['xh'=2,'xl'=2,'yh'=2,'zh'=4,'zl'=4,'yl'=2,'co'=2] {'xh','xl','yh','..., dimensions={0} | all-to-all | bytes 98304 | tf_op jit(solution)/shard_map/all_to_all | solution.py:291
  67.1 13.9 %all_to_all.34.got_ref = f32[16,1,384]{2,1,0:T(1,128)S(1)} all-to-all(f32[16,1,384]{2,1,0:T(1,128)S(1)} %sum_plane.1), channel_id=1, replica_groups=mesh['xh'=2,'xl'=2,'yh'=2,'zh'=4,'zl'=4,'yl'=2,'co'=2] {'zh','zl'}, dimensions={0} | all-to-all | bytes 49152 | tf_op jit(solution)/shard_map/all_to_all | solution.py:291
  81.0 0.0 copy-start
  81.0 12.0 %all_to_all.35.got_ref = f32[32,1,384]{2,1,0:T(1,128)S(1)} all-to-all(f32[32,1,384]{2,1,0:T(1,128)S(1)} %sum_ring.1), channel_id=1, replica_groups=mesh['xh'=2,'xl'=2,'yh'=2,'zh'=4,'zl'=4,'yl'=2,'co'=2] {'xh','xl','yh','..., dimensions={0} | all-to-all | bytes 98304 | tf_op jit(solution)/shard_map/all_to_all | solution.py:291
  93.0 0.0 copy-done
  93.0 0.7 clip.1
  (2 shorter events, 0.1 us)
Async XLA Ops:
  0.6 0.9 copy-start.4
  0.6 0.9 copy-start.1
  0.7 53.5 %copy-start.5 = (bf16[2,25,6000]{2,0,1:T(2,128)(2,1)S(1)}, bf16[2,25,6000]{2,0,1:T(2,128)(2,1)}, u32[]{:S(2)}) copy-start(bf16[2,25,6000]{2,0,1:T(2,128)(2,1)} %param.12) | copy-start | bytes 1800004
  2.0 18.0 %copy-start.2 = (f32[16,25]{1,0:T(8,128)S(1)}, f32[16,25]{1,0:T(8,128)}, u32[]{:S(2)}) copy-start(f32[16,25]{1,0:T(8,128)} %light_ref.1) | copy-start | bytes 4804
  2.0 18.0 %copy-start.3 = (s32[2,16,2]{1,2,0:T(2,128)S(1)}, s32[2,16,2]{1,2,0:T(2,128)}, u32[]{:S(2)}) copy-start(s32[2,16,2]{1,2,0:T(2,128)} %param.8) | copy-start | bytes 772
  81.0 12.0 %copy-start = (s32[6000]{0:T(1024)S(1)}, s32[6000]{0:T(1024)}, u32[]{:S(2)}) copy-start(s32[6000]{0:T(1024)} %code_ref.1) | copy-start | bytes 72004
